TPU v7x, 512 devices: a whole 4x8x8 slice. The times are simulated.
512 devices in a mesh: tm: 16 (over x, z_lo, core), patch: 32 (over y, z_hi).
Axes of the slice: x: 4, y: 8, z: 8 (z_hi: 4, z_lo: 2; z = z_hi * 2 + z_lo), core: 2. Of those that a mesh axis runs over, the one named last changes fastest.
Arguments:
- multiplier: float32 [16, 2, 16, 1024, 128], P('tm', None, None, 'patch'), may hold values from -6 to 6
- obs_multiplier: float32 [16, 32768], P('tm', 'patch'), may hold values from -6 to 6
- increment: float32 [16, 2, 16, 1024, 128], P('tm', None, None, 'patch'), may hold values from -6 to 6
- error_var: float32 [16, 2, 16, 1024, 128], P('tm', None, None, 'patch'), may hold values from 0.25 to 4
- obs_var: float32 [16, 32768], P('tm', 'patch'), may hold values from 0.5 to 2
- div_damping: float32 [16, 2, 16, 1024, 128], P('tm', None, None, 'patch'), may hold values from 0.02 to 0.1
- bih_damping: float32 [16, 2, 16, 1024, 128], P('tm', None, None, 'patch'), may hold values from 0.002 to 0.012
- obs_weight: float32 [16, 2, 16, 32768], P('tm', None, None, 'patch'), may hold values from -1 to 1
- obs_cell: int32 [16, 32768], P('tm', 'patch'), may hold values from 0 to 4095
- edge_map: int32 [32, 128], P('patch'), may hold values from 0 to 127, each once within a row
Outputs:
- model_part: float32 [16, 2, 16, 1024, 128], P('tm', None, None, 'patch')
- obs_part: float32 [16, 32768], P('tm', 'patch')
- state_part: float32 [16, 2, 16, 1024, 128], P('tm', None, None, 'patch')
Inputs may be any that keep to these rules, and one draw needn't show every extreme that they name: `edge_map`: row p lists, for each column of patch p's first row, the column of patch p-1's last row that lies beside it. `obs_cell`: a cell of the observation's own patch, counted as row * 128 + column within the patch.
All inputs are finite; a program needn't handle non-finite values.
Results may differ from a plain program's by a relative error of at most 0.00002.
Values sent between devices are 32-bit elements; how exact they have to be, the bound alone decides.
A program may use at most 64 MiB of HBM per device.

v0:
```python
import functools

import jax
import jax.numpy as jnp
from jax import lax
from jax.experimental import pallas as pl
from jax.experimental.pallas import tpu as pltpu
from jax.sharding import PartitionSpec as P

MESH = pl.DeviceIdType.MESH
HALO = 4
CHUNKS = 4


def dot_nt(a, b):
    return lax.dot_general(a, b, (((1,), (1,)), ((), ())), preferred_element_type=jnp.float32)


def dot_nn(a, b):
    return lax.dot_general(a, b, (((1,), (0,)), ((), ())), preferred_element_type=jnp.float32)


def split(x):
    hi = x.astype(jnp.bfloat16)
    return hi, (x - hi.astype(jnp.float32)).astype(jnp.bfloat16)


def lane_take(tile, index):
    return jnp.take_along_axis(tile, index, axis=1, mode="promise_in_bounds")


def inverse_rows(perm):
    cols = perm.shape[1]
    target = lax.broadcasted_iota(jnp.int32, (cols, cols), 0)
    hot = (jnp.broadcast_to(perm[0:1], (cols, cols)) == target).astype(jnp.float32).astype(jnp.bfloat16)
    source = lax.broadcasted_iota(jnp.int32, perm.shape, 1).astype(jnp.float32).astype(jnp.bfloat16)
    return dot_nt(source, hot).astype(jnp.int32)


class Geometry:
    def __init__(self, rows, cols, perm, inverse, perm_up, inverse_up):
        self.rows, self.total, self.cols = rows, rows + 2 * HALO, cols
        row = lax.broadcasted_iota(jnp.int32, (8, cols), 0)
        lane = lax.broadcasted_iota(jnp.int32, (8, cols), 1)
        self.up_own = jnp.where(row == 7, inverse_up, lane)
        self.up_halo = jnp.where(row == 7, inverse, lane)
        self.down_own = jnp.where(row == 0, perm, lane)
        self.down_halo = jnp.where(row == 0, perm_up, lane)
        lanes = lax.broadcasted_iota(jnp.int32, (self.total, cols), 1)
        self.first = lanes == 0
        self.last = lanes == cols - 1

    def up(self, f):
        g = pltpu.roll(f, self.total - 1, 0)
        r = self.rows
        return jnp.concatenate(
            [g[: r - 8], lane_take(g[r - 8 : r], self.up_own), lane_take(g[r:], self.up_halo)], 0
        )

    def down(self, f):
        g = pltpu.roll(f, 1, 0)
        r = self.rows
        return jnp.concatenate(
            [lane_take(g[:8], self.down_own), g[8:r], lane_take(g[r:], self.down_halo)], 0
        )

    def right(self, f):
        return jnp.where(self.last, f, pltpu.roll(f, self.cols - 1, 1))

    def left(self, f):
        return jnp.where(self.first, f, pltpu.roll(f, 1, 1))

    def column_adjoint(self, f):
        return jnp.where(self.first, 0.0, pltpu.roll(f, 1, 1)) - jnp.where(self.last, 0.0, f)

    def step(self, u, v, a, b):
        up_u = self.up(u)
        right_v = self.right(v)
        lap_u = (up_u + self.down(u)) + (self.right(u) + self.left(u)) - 4.0 * u
        lap_v = (self.up(v) + self.down(v)) + (right_v + self.left(v)) - 4.0 * v
        sdiv = a * ((up_u - u) + (right_v - v))
        su = b * lap_u
        sv = b * lap_v
        lap_su = (self.up(su) + self.down(su)) + (self.right(su) + self.left(su)) - 4.0 * su
        lap_sv = (self.up(sv) + self.down(sv)) + (self.right(sv) + self.left(sv)) - 4.0 * sv
        return u - lap_su - (self.down(sdiv) - sdiv), v - lap_sv - self.column_adjoint(sdiv)


def kernel(
    sizes,
    obsm, obsv, cell, perm, mult_h, inc_h, err_h, div_h, bih_h, w_h,
    model_h, obs_o, state_h,
    mult, inc, err, div, bih, w, prev, bwd, adj, model, state,
    up_s, down_s, inc_up_s, inc_down_s, low_r, high_r, prev_low, prev_high, perm_s, perm_r,
    a_hi, a_lo, wide, hot,
    load_sem, send_sem, recv_sem, store_sem,
):
    levels, rows, cols, count, n_tm, n_patch = sizes
    k, p = lax.axis_index("tm"), lax.axis_index("patch")
    k_next, k_prev = lax.rem(k + 1, n_tm), lax.rem(k + n_tm - 1, n_tm)
    p_next, p_prev = lax.rem(p + 1, n_patch), lax.rem(p + n_patch - 1, n_patch)

    loads = [
        pltpu.make_async_copy(src, dst, load_sem.at[i])
        for i, (src, dst) in enumerate(
            ((mult_h, mult), (div_h, div), (bih_h, bih), (inc_h, inc), (w_h, w), (err_h, err))
        )
    ]
    for load in loads:
        load.start()

    barrier = pltpu.get_barrier_semaphore()
    for peer in ((k, p_next), (k, p_prev), (k_prev, p), (k_next, p), (k_prev, p_next), (k_prev, p_prev)):
        pl.semaphore_signal(barrier, inc=1, device_id=peer, device_id_type=MESH)

    def remote(index, src, dst, peer):
        return pltpu.make_async_remote_copy(
            src_ref=src, dst_ref=dst, send_sem=send_sem.at[index], recv_sem=recv_sem.at[index],
            device_id=peer, device_id_type=MESH,
        )

    perm_s[...] = jnp.broadcast_to(perm[...], perm_s.shape)
    for i, (load, field) in enumerate(zip(loads[:3], (mult, div, bih))):
        load.wait()
        up_s[2 * i : 2 * i + 2] = field[:, :, rows - HALO :, :]
        down_s[2 * i : 2 * i + 2] = field[:, :, :HALO, :]
    pl.semaphore_wait(barrier, 6)
    rims = [
        remote(0, up_s, low_r, (k, p_next)),
        remote(1, down_s, high_r, (k, p_prev)),
        remote(2, perm_s, perm_r, (k, p_prev)),
    ]
    for copy in rims:
        copy.start()
    bulk = remote(3, inc_h, prev, (k_next, p))
    bulk.start()
    loads[3].wait()
    inc_up_s[...] = inc[:, :, rows - HALO :, :]
    inc_down_s[...] = inc[:, :, :HALO, :]
    inc_rims = [
        remote(4, inc_up_s, prev_low, (k_next, p_next)),
        remote(5, inc_down_s, prev_high, (k_next, p_prev)),
    ]
    for copy in inc_rims:
        copy.start()

    half = rows // 2
    cells = cell[...]
    row = cells // cols
    within = (row // half) * cols + cells % cols
    group = row % half
    hot[...] = (
        lax.broadcasted_iota(jnp.int32, (2 * cols, count), 0) == jnp.broadcast_to(within, (2 * cols, count))
    ).astype(jnp.float32).astype(jnp.bfloat16)
    mask = lax.broadcasted_iota(jnp.int32, (half, count), 0) == jnp.broadcast_to(group, (half, count))
    loads[4].wait()
    loads[5].wait()
    times = obsm[...]
    for var in range(2):
        for lev in range(levels):
            at = (var * levels + lev) * half
            weight = w[var * levels + lev : var * levels + lev + 1, :]
            hi, lo = split(jnp.where(mask, jnp.broadcast_to(weight * times, mask.shape), 0.0))
            a_hi[at : at + half] = hi
            a_lo[at : at + half] = lo
            plane = inc[var, lev]
            hi, lo = split(jnp.concatenate([plane[:half], plane[half:]], 1))
            wide[at : at + half, : 2 * cols] = hi
            wide[at : at + half, 2 * cols :] = lo
    block = min(256, count)
    for start in range(0, count, block):
        part = hot[:, start : start + block]
        found = dot_nn(wide[...], jnp.concatenate([part, part], 0))
        found = found.reshape(2 * levels, half, block)
        found = jnp.where(mask[None, :, start : start + block], found, 0.0)
        found = jnp.sum(found.reshape(2 * levels, half // 8, 8, block), 1)
        found = found * w[:, start : start + block][:, None, :]
        found = jnp.sum(jnp.sum(found, 0), 0, keepdims=True)
        span = pl.ds(start, block)
        obs_o[:, span] = obsv[:, span] * obsm[:, span] + found
    spread = dot_nt(a_hi[...], hot[...]) + dot_nt(a_lo[...], hot[...])
    spread = spread.reshape(2, levels, half, 2 * cols)
    state[:, :, :half, :] = mult[:, :, :half, :] + spread[..., :cols]
    state[:, :, half:, :] = mult[:, :, half:, :] + spread[..., cols:]

    for copy in rims:
        copy.wait()
    own = jnp.broadcast_to(perm[...], perm_r.shape)
    above = perm_r[...]
    geo = Geometry(rows, cols, own, inverse_rows(own), above, inverse_rows(above))

    def whole(field, high, low):
        return jnp.concatenate([field, high, low], 0)

    def coefs(lev, s):
        return (
            whole(div[s, lev], high_r[2 + s, lev], low_r[2 + s, lev]),
            whole(bih[s, lev], high_r[4 + s, lev], low_r[4 + s, lev]),
        )

    per = levels // CHUNKS
    back = []
    for chunk in range(CHUNKS):
        def body(i, _, chunk=chunk):
            lev = chunk * per + i
            u = whole(mult[0, lev], high_r[0, lev], low_r[0, lev])
            v = whole(mult[1, lev], high_r[1, lev], low_r[1, lev])
            for s in (1, 0):
                u, v = geo.step(u, v, *coefs(lev, s))
            adj[0, lev] = u[:rows]
            adj[1, lev] = v[:rows]
            return 0

        lax.fori_loop(0, per, body, 0)
        span = pl.ds(chunk * per, per)
        copy = remote(6 + chunk, adj.at[:, span], bwd.at[:, span], (k_prev, p))
        copy.start()
        back.append(copy)

    bulk.wait()
    for copy in inc_rims:
        copy.wait()
    stores = []
    for chunk in range(CHUNKS):
        def body(i, _, chunk=chunk):
            lev = chunk * per + i
            u = whole(prev[0, lev], prev_high[0, lev], prev_low[0, lev])
            v = whole(prev[1, lev], prev_high[1, lev], prev_low[1, lev])
            for s in (0, 1):
                u, v = geo.step(u, v, *coefs(lev, s))
            for var, f in ((0, u), (1, v)):
                forward = jnp.where(k == 0, 0.0, f[:rows])
                model[var, lev] = err[var, lev] * mult[var, lev] + inc[var, lev] - forward
            return 0

        lax.fori_loop(0, per, body, 0)
        span = pl.ds(chunk * per, per)
        copy = pltpu.make_async_copy(model.at[:, span], model_h.at[:, span], store_sem.at[chunk])
        copy.start()
        stores.append(copy)
    for chunk in range(CHUNKS):
        back[chunk].wait()
        span = pl.ds(chunk * per, per)
        state[:, span] = state[:, span] - jnp.where(k == n_tm - 1, 0.0, bwd[:, span])
        copy = pltpu.make_async_copy(state.at[:, span], state_h.at[:, span], store_sem.at[CHUNKS + chunk])
        copy.start()
        stores.append(copy)
    for copy in stores:
        copy.wait()


def solution(mesh):
    n_tm, n_patch = mesh.shape["tm"], mesh.shape["patch"]

    def per_device(mult, obsm, inc, err, obsv, div, bih, w, cell, perm):
        _, _, levels, rows, cols = mult.shape
        count = obsm.shape[1]
        whole = (2, levels, rows, cols)
        rim = (2, levels, HALO, cols)
        f32 = functools.partial(pltpu.VMEM, dtype=jnp.float32)
        scratch = [f32(whole)] * 5 + [f32((2 * levels, count))] + [f32(whole)] * 5
        scratch += [f32((6,) + rim[1:])] * 2 + [f32(rim)] * 2
        scratch += [f32((6,) + rim[1:])] * 2 + [f32(rim)] * 2
        scratch += [pltpu.VMEM((8, cols), jnp.int32)] * 2
        tall = 2 * levels * (rows // 2)
        scratch += [
            pltpu.VMEM((tall, count), jnp.bfloat16),
            pltpu.VMEM((tall, count), jnp.bfloat16),
            pltpu.VMEM((tall, 4 * cols), jnp.bfloat16),
            pltpu.VMEM((2 * cols, count), jnp.bfloat16),
        ]
        scratch += [
            pltpu.SemaphoreType.DMA((6,)),
            pltpu.SemaphoreType.DMA((6 + CHUNKS,)),
            pltpu.SemaphoreType.DMA((6 + CHUNKS,)),
            pltpu.SemaphoreType.DMA((2 * CHUNKS,)),
        ]
        vmem, any_ = pl.BlockSpec(memory_space=pltpu.VMEM), pl.BlockSpec(memory_space=pltpu.HBM)
        model, obs, state = pl.pallas_call(
            functools.partial(kernel, (levels, rows, cols, count, n_tm, n_patch)),
            out_shape=(
                jax.ShapeDtypeStruct(whole, jnp.float32),
                jax.ShapeDtypeStruct((1, count), jnp.float32),
                jax.ShapeDtypeStruct(whole, jnp.float32),
            ),
            in_specs=[vmem] * 4 + [any_] * 6,
            out_specs=(any_, vmem, any_),
            scratch_shapes=scratch,
            compiler_params=pltpu.CompilerParams(
                collective_id=0, has_side_effects=True, vmem_limit_bytes=48 * 1024 * 1024
            ),
        )(
            obsm, obsv, cell, perm, mult.reshape(whole), inc.reshape(whole), err.reshape(whole),
            div.reshape(whole), bih.reshape(whole), w.reshape(2 * levels, count),
        )
        return model[None], obs, state[None]

    field = P("tm", None, None, "patch", None)
    per_obs = P("tm", "patch")
    return jax.shard_map(
        per_device,
        mesh=mesh,
        in_specs=(
            field, per_obs, field, field, per_obs, field, field,
            P("tm", None, None, "patch"), per_obs, P("patch", None),
        ),
        out_specs=(field, per_obs, field),
        check_vma=False,
    )
```

profile of v0, /device:TPU:56, one launch (start us, length us, event | category | flops | bytes accessed | tf_op | source)
XLA Modules:
  0.0 54.6 jit_solution(17773854052333411520)
XLA Ops:
  0.6 0.0 copy-start.7
  0.6 0.0 copy-start.6
  0.7 0.0 copy-start.9
  0.7 0.7 %copy-done.7 = f32[1,1024]{1,0:T(1,128)S(1)} copy-done((f32[1,1024]{1,0:T(1,128)S(1)}, f32[1,1024]{1,0:T(1,128)}, u32[]{:S(2)}) %copy-start.7) | copy-done | bytes 4120
  1.3 0.0 copy-done.6
  1.3 0.0 copy-done.9
  1.3 0.0 copy-start
  1.3 1.0 %copy-done = f32[1,2,16,32,128]{4,3,2,1,0:T(8,128)S(1)} copy-done((f32[1,2,16,32,128]{4,3,2,1,0:T(8,128)S(1)}, f32[1,2,16,32,128]{4,3,2,1,0:T(8,128)}, u32[]{:S(2)}) %copy-start) | copy-done | bytes 524312
  2.4 0.0 copy-start.1
  2.4 1.0 %copy-done.1 = f32[1,2,16,32,128]{4,3,2,1,0:T(8,128)S(1)} copy-done((f32[1,2,16,32,128]{4,3,2,1,0:T(8,128)S(1)}, f32[1,2,16,32,128]{4,3,2,1,0:T(8,128)}, u32[]{:S(2)}) %copy-start.1) | copy-done | bytes 524312
  3.4 0.0 copy-start.2
  3.4 1.0 %copy-done.2 = f32[1,2,16,32,128]{4,3,2,1,0:T(8,128)S(1)} copy-done((f32[1,2,16,32,128]{4,3,2,1,0:T(8,128)S(1)}, f32[1,2,16,32,128]{4,3,2,1,0:T(8,128)}, u32[]{:S(2)}) %copy-start.2) | copy-done | bytes 524312
  4.5 0.0 copy-start.3
  4.5 1.0 %copy-done.3 = f32[1,2,16,32,128]{4,3,2,1,0:T(8,128)S(1)} copy-done((f32[1,2,16,32,128]{4,3,2,1,0:T(8,128)S(1)}, f32[1,2,16,32,128]{4,3,2,1,0:T(8,128)}, u32[]{:S(2)}) %copy-start.3) | copy-done | bytes 524312
  5.5 0.0 copy-start.4
  5.5 1.0 %copy-done.4 = f32[1,2,16,32,128]{4,3,2,1,0:T(8,128)S(1)} copy-done((f32[1,2,16,32,128]{4,3,2,1,0:T(8,128)S(1)}, f32[1,2,16,32,128]{4,3,2,1,0:T(8,128)}, u32[]{:S(2)}) %copy-start.4) | copy-done | bytes 524312
  6.6 0.0 copy-start.5
  6.6 0.9 %copy-done.5 = f32[1,2,16,1024]{3,2,1,0:T(8,128)S(1)} copy-done((f32[1,2,16,1024]{3,2,1,0:T(8,128)S(1)}, f32[1,2,16,1024]{3,2,1,0:T(8,128)}, u32[]{:S(2)}) %copy-start.5) | copy-done | bytes 131096
  7.5 0.0 copy-start.8
  7.5 0.7 %copy-done.8 = s32[1,1024]{1,0:T(1,128)S(1)} copy-done((s32[1,1024]{1,0:T(1,128)S(1)}, s32[1,1024]{1,0:T(1,128)}, u32[]{:S(2)}) %copy-start.8) | copy-done | bytes 4120
  8.1 44.2 %shard_map.121 = (f32[2,16,32,128]{3,2,1,0:T(8,128)S(1)}, f32[1,1024]{1,0:T(1,128)S(1)}, f32[2,16,32,128]{3,2,1,0:T(8,128)S(1)}) custom-call(f32[1,1024]{1,0:T(1,128)S(1)} %copy-done.6, f32[1,1024]{1,0:T(1,128)S(1)} %copy-done.7, s32[1,1024]{1,0:T(1,128)S(1)} %copy-done.8, s32[1,128]{1,0:T(1,128)S(1)} %copy-done.9, f32[2,16,32,128]{3,2,1,0:T(8,128)S(1)} %bitcast.10, ...), custom_call_target="tpu_custom_call" | custom-call | tf_op jit(solution)/shard_map/pallas_call | solution.py:279
  52.4 0.8 %copy.16 = f32[1,2,16,32,128]{4,3,2,1,0:T(8,128)} copy(f32[1,2,16,32,128]{4,3,2,1,0:T(8,128)S(1)} %bitcast.9) | data formatting | bytes 1048576
  53.2 0.6 %copy.17 = f32[1,1024]{1,0:T(1,128)} copy(f32[1,1024]{1,0:T(1,128)S(1)} %get-tuple-element.13) | data formatting | bytes 8192
  53.8 0.8 %copy.18 = f32[1,2,16,32,128]{4,3,2,1,0:T(8,128)} copy(f32[1,2,16,32,128]{4,3,2,1,0:T(8,128)S(1)} %bitcast.8) | data formatting | bytes 1048576
Async XLA Ops:
  0.6 0.7 %copy-start.7 = (f32[1,1024]{1,0:T(1,128)S(1)}, f32[1,1024]{1,0:T(1,128)}, u32[]{:S(2)}) copy-start(f32[1,1024]{1,0:T(1,128)} %obsv.1) | copy-start | bytes 12292
  0.6 0.7 %copy-start.6 = (f32[1,1024]{1,0:T(1,128)S(1)}, f32[1,1024]{1,0:T(1,128)}, u32[]{:S(2)}) copy-start(f32[1,1024]{1,0:T(1,128)} %obsm.1) | copy-start | bytes 12292
  0.7 0.7 %copy-start.9 = (s32[1,128]{1,0:T(1,128)S(1)}, s32[1,128]{1,0:T(1,128)}, u32[]{:S(2)}) copy-start(s32[1,128]{1,0:T(1,128)} %perm.1) | copy-start | bytes 1540
  1.3 1.0 %copy-start = (f32[1,2,16,32,128]{4,3,2,1,0:T(8,128)S(1)}, f32[1,2,16,32,128]{4,3,2,1,0:T(8,128)}, u32[]{:S(2)}) copy-start(f32[1,2,16,32,128]{4,3,2,1,0:T(8,128)} %param.10) | copy-start | bytes 1572868
  2.4 1.0 %copy-start.1 = (f32[1,2,16,32,128]{4,3,2,1,0:T(8,128)S(1)}, f32[1,2,16,32,128]{4,3,2,1,0:T(8,128)}, u32[]{:S(2)}) copy-start(f32[1,2,16,32,128]{4,3,2,1,0:T(8,128)} %param.12) | copy-start | bytes 1572868
  3.4 1.0 %copy-start.2 = (f32[1,2,16,32,128]{4,3,2,1,0:T(8,128)S(1)}, f32[1,2,16,32,128]{4,3,2,1,0:T(8,128)}, u32[]{:S(2)}) copy-start(f32[1,2,16,32,128]{4,3,2,1,0:T(8,128)} %param.13) | copy-start | bytes 1572868
  4.5 1.0 %copy-start.3 = (f32[1,2,16,32,128]{4,3,2,1,0:T(8,128)S(1)}, f32[1,2,16,32,128]{4,3,2,1,0:T(8,128)}, u32[]{:S(2)}) copy-start(f32[1,2,16,32,128]{4,3,2,1,0:T(8,128)} %param.15) | copy-start | bytes 1572868
  5.5 1.0 %copy-start.4 = (f32[1,2,16,32,128]{4,3,2,1,0:T(8,128)S(1)}, f32[1,2,16,32,128]{4,3,2,1,0:T(8,128)}, u32[]{:S(2)}) copy-start(f32[1,2,16,32,128]{4,3,2,1,0:T(8,128)} %param.16) | copy-start | bytes 1572868
  6.6 0.9 %copy-start.5 = (f32[1,2,16,1024]{3,2,1,0:T(8,128)S(1)}, f32[1,2,16,1024]{3,2,1,0:T(8,128)}, u32[]{:S(2)}) copy-start(f32[1,2,16,1024]{3,2,1,0:T(8,128)} %param.17) | copy-start | bytes 393220
  7.5 0.7 %copy-start.8 = (s32[1,1024]{1,0:T(1,128)S(1)}, s32[1,1024]{1,0:T(1,128)}, u32[]{:S(2)}) copy-start(s32[1,1024]{1,0:T(1,128)} %cell.1) | copy-start | bytes 12292
where the time goes:
time: 55 us; the launch traced here: 54.6 us
  Pallas kernels  44.2 us (80%)
  local copies, waits for them, and re-layouts  9.66 us (18%)
  between operations  0.68 us (1%)
    pallas_call x1, Pallas kernels, per_device(): pl.pallas_call(functools.partial(kernel, (levels, rows, cols, count, n_tm...  44.2 us
    unnamed x23, local copies, waits for them, and re-layouts  9.66 us

commit v1 on v0

v1 whole, which is shorter than its diff:
```python
import functools

import jax
import jax.numpy as jnp
from jax import lax
from jax.experimental import pallas as pl
from jax.experimental.pallas import tpu as pltpu
from jax.sharding import PartitionSpec as P

MESH = pl.DeviceIdType.MESH
HALO = 4
CHUNKS = 4


def dot_nt(a, b):
    return lax.dot_general(a, b, (((1,), (1,)), ((), ())), preferred_element_type=jnp.float32)


def dot_nn(a, b):
    return lax.dot_general(a, b, (((1,), (0,)), ((), ())), preferred_element_type=jnp.float32)


def split(x):
    hi = x.astype(jnp.bfloat16)
    return hi, (x - hi.astype(jnp.float32)).astype(jnp.bfloat16)


def inverse_rows(perm):
    cols = perm.shape[1]
    target = lax.broadcasted_iota(jnp.int32, (cols, cols), 0)
    hot = (jnp.broadcast_to(perm[0:1], (cols, cols)) == target).astype(jnp.float32).astype(jnp.bfloat16)
    source = lax.broadcasted_iota(jnp.int32, perm.shape, 1).astype(jnp.float32).astype(jnp.bfloat16)
    return dot_nt(source, hot).astype(jnp.int32)


def lane_take(tile, index):
    return jnp.take_along_axis(tile, index, axis=1, mode="promise_in_bounds")

class Stencil:
    def __init__(self, cols):
        self.cols = cols
        self.row = lax.broadcasted_iota(jnp.int32, (8, cols), 0)
        self.lane = lax.broadcasted_iota(jnp.int32, (8, cols), 1)
        self.first, self.last = self.lane == 0, self.lane == cols - 1
        self.top, self.bottom = self.row == 7, self.row == 0
        self.low_side, self.high_side = self.row == 3, self.row == 4

    def up(self, tiles):
        r = [pltpu.roll(t, 7, 0) for t in tiles]
        return [jnp.where(self.top, r[(i + 1) % len(r)], r[i]) for i in range(len(r))]

    def down(self, tiles):
        r = [pltpu.roll(t, 1, 0) for t in tiles]
        return [jnp.where(self.bottom, r[i - 1], r[i]) for i in range(len(r))]

    def rows_around(self, tiles, seams):
        above, below = list(tiles), list(tiles)
        for i, index in seams:
            crossed = lane_take(tiles[i], index)
            above[i] = jnp.where(self.high_side, crossed, tiles[i])
            below[i] = jnp.where(self.low_side, crossed, tiles[i])
        return self.up(above), self.down(below)

    def right(self, tiles):
        return [jnp.where(self.last, t, pltpu.roll(t, self.cols - 1, 1)) for t in tiles]

    def left(self, tiles):
        return [jnp.where(self.first, t, pltpu.roll(t, 1, 1)) for t in tiles]

    def lap(self, f, above, below, right):
        return [(a + b) + (r + l) - 4.0 * t for t, a, b, r, l in zip(f, above, below, right, self.left(f))]

    def step(self, u, v, a, b, seams):
        up_u, down_u = self.rows_around(u, seams)
        up_v, down_v = self.rows_around(v, seams)
        right_v = self.right(v)
        sdiv = [c * ((q - p) + (s - r)) for c, p, q, r, s in zip(a, u, up_u, v, right_v)]
        su = [c * t for c, t in zip(b, self.lap(u, up_u, down_u, self.right(u)))]
        sv = [c * t for c, t in zip(b, self.lap(v, up_v, down_v, right_v))]
        lap_su = self.lap(su, *self.rows_around(su, seams), self.right(su))
        lap_sv = self.lap(sv, *self.rows_around(sv, seams), self.right(sv))
        below = self.rows_around(sdiv, seams)[1]
        out_u = [t - l - (q - d) for t, l, q, d in zip(u, lap_su, below, sdiv)]
        out_v = [
            t - l - (jnp.where(self.first, 0.0, pltpu.roll(d, 1, 1)) - jnp.where(self.last, 0.0, d))
            for t, l, d in zip(v, lap_sv, sdiv)
        ]
        return out_u, out_v

    def shift(self, x, y):
        return jnp.where(self.row < 4, pltpu.roll(x, 4, 0), pltpu.roll(y, 4, 0))


def kernel(
    sizes,
    obsm, obsv, cell, perm, mult_h, inc_h, err_h, div_h, bih_h, w_h,
    model_h, obs_o, state_h,
    model, state, mult, inc, err, div, bih, w, prev,
    adj_in, adj_ed, bwd_in, bwd_ed,
    up_s, down_s, inc_up_s, inc_down_s, low_r, high_r, prev_low, prev_high, perm_s, perm_r,
    a_hi, a_lo, wide, hot,
    load_sem, send_sem, recv_sem, store_sem, note_sem,
):
    levels, rows, cols, count, n_tm, n_patch = sizes
    per = levels // CHUNKS
    k, p = lax.axis_index("tm"), lax.axis_index("patch")
    k_next, k_prev = lax.rem(k + 1, n_tm), lax.rem(k + n_tm - 1, n_tm)
    p_next, p_prev = lax.rem(p + 1, n_patch), lax.rem(p + n_patch - 1, n_patch)
    even = lax.rem(p, 2) == 0
    odd = lax.rem(p, 2) == 1
    first = lax.rem(p, 4) == 0
    later = lax.rem(p, 4) != 0

    loads = [
        pltpu.make_async_copy(src, dst, load_sem.at[i])
        for i, (src, dst) in enumerate(
            ((mult_h, mult), (div_h, div), (bih_h, bih), (inc_h, inc), (w_h, w), (err_h, err))
        )
    ]
    for load in loads:
        load.start()

    def remote(index, src, dst, peer):
        return pltpu.make_async_remote_copy(
            src_ref=src, dst_ref=dst, send_sem=send_sem.at[index], recv_sem=recv_sem.at[index],
            device_id=peer, device_id_type=MESH,
        )

    def note(index, peer):
        pl.semaphore_signal(note_sem.at[index], inc=1, device_id=peer, device_id_type=MESH)

    RIM_UP, RIM_DOWN, BACK_IN, BACK_ED, BULK, INC_UP, INC_DOWN, PERM = (i * CHUNKS for i in range(8))
    FROM_ABOVE, FROM_BELOW, BESIDE_ABOVE, BESIDE_BELOW, GO_ABOVE, GO_BELOW = range(6)

    def rim_up(c):
        return remote(RIM_UP + c, up_s.at[c], low_r.at[c], (k, p_next))

    def rim_down(c):
        return remote(RIM_DOWN + c, down_s.at[c], high_r.at[c], (k, p_prev))

    def back_in(c):
        span = pl.ds(c * per, per)
        return remote(BACK_IN + c, adj_in.at[:, span], bwd_in.at[:, span], (k_prev, p))

    def back_ed(c):
        span = pl.ds(c * per, per)
        return remote(BACK_ED + c, adj_ed.at[:, span], bwd_ed.at[:, span], (k_prev, p))

    send_perm = remote(PERM, perm_s, perm_r, (k, p_prev))

    def bulk(c):
        span = pl.ds(c * per, per)
        return remote(BULK + c, inc_h.at[:, span], prev.at[:, span], (k_next, p))

    def inc_up(c):
        return remote(INC_UP + c, inc_up_s.at[c], prev_low.at[c], (k_next, p_next))

    def inc_down(c):
        return remote(INC_DOWN + c, inc_down_s.at[c], prev_high.at[c], (k_next, p_prev))

    def start_all(*copies):
        for copy in copies:
            for c in range(CHUNKS):
                copy(c).start()

    barrier = pltpu.get_barrier_semaphore()

    @pl.when(even)
    def _():
        for peer in ((k_prev, p), (k_next, p), (k, p_prev), (k, p_next)):
            pl.semaphore_signal(barrier, inc=1, device_id=peer, device_id_type=MESH)

    pl.semaphore_wait(barrier, 2)

    @pl.when(odd)
    def _():
        note(FROM_ABOVE, (k, p_prev))
        note(FROM_BELOW, (k, p_next))

    @pl.when(even)
    def _():
        start_all(bulk)

    st = Stencil(cols)
    perm_s[...] = jnp.broadcast_to(perm[...], perm_s.shape)
    for load in loads[:3]:
        load.wait()

    def pack(c, _):
        span = pl.ds(c * per, per)
        for var in range(2):
            up_s[c, var] = mult[var, span, rows - HALO :, :]
            down_s[c, var] = mult[var, span, :HALO, :]
        for i, coef in enumerate((div.at[0], div.at[1], bih.at[0])):
            up_s[c, 2 + i, :, 1:, :] = coef[span, rows - 3 :, :]
            up_s[c, 2 + i, :, :1, :] = bih[1, span, rows - 3 + i : rows - 2 + i, :]
            down_s[c, 2 + i, :, :3, :] = coef[span, :3, :]
            down_s[c, 2 + i, :, 3:, :] = bih[1, span, i : i + 1, :]
        return 0

    lax.fori_loop(0, CHUNKS, pack, 0)

    def send_up():
        start_all(rim_up)

    def send_down():
        send_perm.start()
        start_all(rim_down)

    @pl.when(odd)
    def _():
        send_up()
        send_down()

    loads[3].wait()

    def pack_inc(c, _):
        span = pl.ds(c * per, per)
        inc_up_s[c] = inc[:, span, rows - HALO :, :]
        inc_down_s[c] = inc[:, span, :HALO, :]
        return 0

    lax.fori_loop(0, CHUNKS, pack_inc, 0)

    def inner(field, lev):
        return [field[lev, HALO + 8 * i : HALO + 8 * (i + 1), :] for i in range(rows // 8 - 1)]

    def adjoint_inside(c, _):
        for g in range(per):
            lev = c * per + g
            u, v = inner(mult.at[0], lev), inner(mult.at[1], lev)
            for s in (1, 0):
                u, v = st.step(u, v, inner(div.at[s], lev), inner(bih.at[s], lev), ())
            for var, f in ((0, u), (1, v)):
                for i in range(rows // 8 - 2):
                    adj_in[var, lev, 8 * i : 8 * (i + 1), :] = st.shift(f[i], f[i + 1])

        @pl.when(even)
        def _():
            back_in(c).start()

        return 0

    @pl.when(first)
    def _():
        lax.fori_loop(0, CHUNKS, adjoint_inside, 0)

    @pl.when(even)
    def _():
        pl.semaphore_wait(note_sem.at[FROM_ABOVE], 1)
        send_up()
        note(BESIDE_ABOVE, (k_prev, p))
        note(BESIDE_ABOVE, (k_next, p))
        pl.semaphore_wait(note_sem.at[FROM_BELOW], 1)
        send_down()
        note(BESIDE_BELOW, (k_prev, p))
        note(BESIDE_BELOW, (k_next, p))
        pl.semaphore_wait(note_sem.at[BESIDE_ABOVE], 2)
        note(GO_BELOW, (k, p_next))
        start_all(inc_up)
        pl.semaphore_wait(note_sem.at[BESIDE_BELOW], 2)
        note(GO_ABOVE, (k, p_prev))
        start_all(inc_down)

    @pl.when(odd)
    def _():
        pl.semaphore_wait(note_sem.at[GO_BELOW], 1)
        pl.semaphore_wait(note_sem.at[GO_ABOVE], 1)
        start_all(inc_up, inc_down)

    @pl.when(later)
    def _():
        lax.fori_loop(0, CHUNKS, adjoint_inside, 0)

    half = rows // 2
    cells = cell[...]
    row = cells // cols
    within = (row // half) * cols + cells % cols
    group = row % half
    hot[...] = (
        lax.broadcasted_iota(jnp.int32, (2 * cols, count), 0) == jnp.broadcast_to(within, (2 * cols, count))
    ).astype(jnp.float32).astype(jnp.bfloat16)
    mask = lax.broadcasted_iota(jnp.int32, (half, count), 0) == jnp.broadcast_to(group, (half, count))
    loads[4].wait()
    loads[5].wait()
    times = obsm[...]
    for var in range(2):
        for lev in range(levels):
            at = (var * levels + lev) * half
            weight = w[var * levels + lev : var * levels + lev + 1, :]
            hi, lo = split(jnp.where(mask, jnp.broadcast_to(weight * times, mask.shape), 0.0))
            a_hi[at : at + half] = hi
            a_lo[at : at + half] = lo
            plane = inc[var, lev]
            hi, lo = split(jnp.concatenate([plane[:half], plane[half:]], 1))
            wide[at : at + half, : 2 * cols] = hi
            wide[at : at + half, 2 * cols :] = lo
    block = min(256, count)
    for start in range(0, count, block):
        part = hot[:, start : start + block]
        found = dot_nn(wide[...], jnp.concatenate([part, part], 0))
        found = found.reshape(2 * levels, half, block)
        found = jnp.where(mask[None, :, start : start + block], found, 0.0)
        found = jnp.sum(found.reshape(2 * levels, half // 8, 8, block), 1)
        found = found * w[:, start : start + block][:, None, :]
        found = jnp.sum(jnp.sum(found, 0), 0, keepdims=True)
        span = pl.ds(start, block)
        obs_o[:, span] = obsv[:, span] * obsm[:, span] + found
    spread = dot_nt(a_hi[...], hot[...]) + dot_nt(a_lo[...], hot[...])
    spread = spread.reshape(2, levels, half, 2 * cols)
    state[:, :, :half, :] = mult[:, :, :half, :] + spread[..., :cols]
    state[:, :, half:, :] = mult[:, :, half:, :] + spread[..., cols:]

    @pl.when(odd)
    def _():
        start_all(bulk)

    def keep(var, lev, at, f):
        span = slice(at, at + 8)
        rest = err[var, lev, span, :] * mult[var, lev, span, :] + inc[var, lev, span, :]
        model[var, lev, span, :] = rest - jnp.where(k == 0, 0.0, f)

    def forward_inside(c, _):
        bulk(c).wait_recv()
        for g in range(per):
            lev = c * per + g
            u, v = inner(prev.at[0], lev), inner(prev.at[1], lev)
            for s in (0, 1):
                u, v = st.step(u, v, inner(div.at[s], lev), inner(bih.at[s], lev), ())
            for var, f in ((0, u), (1, v)):
                for i in range(rows // 8 - 2):
                    keep(var, lev, 8 * (i + 1), st.shift(f[i], f[i + 1]))
        return 0

    def all_forward_inside():
        lax.fori_loop(0, CHUNKS, forward_inside, 0)

    @pl.when(even)
    def _():
        all_forward_inside()

    def border(field, high, low, lev):
        return [
            field[lev, rows - 12 : rows - 4, :],
            jnp.concatenate([field[lev, rows - 4 :, :], high], 0),
            jnp.concatenate([low, field[lev, :4, :]], 0),
            field[lev, 4:12, :],
        ]

    def coefs(c, g, s):
        lev = c * per + g
        a = border(div.at[s], high_r[c, 2 + s, g], low_r[c, 2 + s, g], lev)
        if s == 0:
            high, low = high_r[c, 4, g], low_r[c, 4, g]
        else:
            high = jnp.concatenate([high_r[c, 2 + min(i, 2), g, 3:, :] for i in range(4)], 0)
            low = jnp.concatenate([low_r[c, 2 + max(i - 1, 0), g, :1, :] for i in range(4)], 0)
        return a, border(bih.at[s], high, low, lev)

    send_perm.wait_recv()
    own, above = perm_s[...], perm_r[...]

    def seam(low_index, high_index):
        return jnp.where(st.low_side, low_index, jnp.where(st.high_side, high_index, st.lane))

    seams = ((1, seam(above, inverse_rows(above))), (2, seam(own, inverse_rows(own))))

    def adjoint_border(c, _):
        rim_up(c).wait_recv()
        rim_down(c).wait_recv()
        for g in range(per):
            lev = c * per + g
            u, v = (border(mult.at[var], high_r[c, var, g], low_r[c, var, g], lev) for var in range(2))
            for s in (1, 0):
                u, v = st.step(u, v, *coefs(c, g, s), seams)
            for var, f in ((0, u), (1, v)):
                adj_ed[var, lev, :8, :] = st.shift(f[0], f[1])
                adj_ed[var, lev, 8:, :] = st.shift(f[2], f[3])

        @pl.when(odd)
        def _():
            back_in(c).start()

        back_ed(c).start()
        return 0

    lax.fori_loop(0, CHUNKS, adjoint_border, 0)

    @pl.when(odd)
    def _():
        all_forward_inside()

    def model_out(c):
        span = pl.ds(c * per, per)
        return pltpu.make_async_copy(model.at[:, span], model_h.at[:, span], store_sem.at[c])

    def state_out(c):
        span = pl.ds(c * per, per)
        return pltpu.make_async_copy(state.at[:, span], state_h.at[:, span], store_sem.at[CHUNKS + c])

    def forward_border(c, _):
        inc_up(c).wait_recv()
        inc_down(c).wait_recv()
        for g in range(per):
            lev = c * per + g
            u, v = (border(prev.at[var], prev_high[c, var, g], prev_low[c, var, g], lev) for var in range(2))
            for s in (0, 1):
                u, v = st.step(u, v, *coefs(c, g, s), seams)
            for var, f in ((0, u), (1, v)):
                keep(var, lev, rows - 8, st.shift(f[0], f[1]))
                keep(var, lev, 0, st.shift(f[2], f[3]))
        model_out(c).start()
        return 0

    lax.fori_loop(0, CHUNKS, forward_border, 0)
    is_last = k == n_tm - 1

    def finish(c, _):
        span = pl.ds(c * per, per)
        back_in(c).wait_recv()
        inside = pl.ds(8, rows - 16)
        state[:, span, inside, :] = state[:, span, inside, :] - jnp.where(is_last, 0.0, bwd_in[:, span])
        back_ed(c).wait_recv()
        for at, place in ((rows - 8, 0), (0, 8)):
            part = bwd_ed[:, span, place : place + 8, :]
            state[:, span, at : at + 8, :] = state[:, span, at : at + 8, :] - jnp.where(is_last, 0.0, part)
        state_out(c).start()
        return 0

    lax.fori_loop(0, CHUNKS, finish, 0)

    def sent(c, _):
        for copy in (rim_up(c), rim_down(c), back_in(c), back_ed(c), bulk(c), inc_up(c), inc_down(c)):
            copy.wait_send()
        model_out(c).wait()
        state_out(c).wait()
        return 0

    lax.fori_loop(0, CHUNKS, sent, 0)
    send_perm.wait_send()


def hand_over(model_i, obs_i, state_i, model_o, obs_o, state_o, model, obs, state, sems):
    per = model.shape[1] // CHUNKS
    routes = [(obs_i, obs, obs_o)]
    for c in range(CHUNKS):
        span = pl.ds(c * per, per)
        routes.append((model_i.at[:, span], model.at[:, span], model_o.at[:, span]))
        routes.append((state_i.at[:, span], state.at[:, span], state_o.at[:, span]))
    ins = [pltpu.make_async_copy(a, b, sems.at[i]) for i, (a, b, _) in enumerate(routes)]
    outs = [pltpu.make_async_copy(b, c, sems.at[len(routes) + i]) for i, (_, b, c) in enumerate(routes)]
    for copy in ins:
        copy.start()
    for came, goes in zip(ins, outs):
        came.wait()
        goes.start()
    for copy in outs:
        copy.wait()


def solution(mesh):
    n_tm, n_patch = mesh.shape["tm"], mesh.shape["patch"]

    def per_device(mult, obsm, inc, err, obsv, div, bih, w, cell, perm):
        _, _, levels, rows, cols = mult.shape
        count = obsm.shape[1]
        per = levels // CHUNKS
        whole = (2, levels, rows, cols)
        rim = (CHUNKS, 2, per, HALO, cols)
        rims = (CHUNKS, 5, per, HALO, cols)
        f32 = functools.partial(pltpu.VMEM, dtype=jnp.float32)
        scratch = [f32(whole)] * 7 + [f32((2 * levels, count)), f32(whole)]
        scratch += [f32((2, levels, rows - 16, cols)), f32((2, levels, 16, cols))] * 2
        scratch += [f32(rims)] * 2 + [f32(rim)] * 2
        scratch += [f32(rims)] * 2 + [f32(rim)] * 2
        scratch += [pltpu.VMEM((8, cols), jnp.int32)] * 2
        tall = 2 * levels * (rows // 2)
        scratch += [
            pltpu.VMEM((tall, count), jnp.bfloat16),
            pltpu.VMEM((tall, count), jnp.bfloat16),
            pltpu.VMEM((tall, 4 * cols), jnp.bfloat16),
            pltpu.VMEM((2 * cols, count), jnp.bfloat16),
        ]
        copies = 7 * CHUNKS + 1
        scratch += [
            pltpu.SemaphoreType.DMA((6,)),
            pltpu.SemaphoreType.DMA((copies,)),
            pltpu.SemaphoreType.DMA((copies,)),
            pltpu.SemaphoreType.DMA((2 * CHUNKS,)),
            pltpu.SemaphoreType.REGULAR((6,)),
        ]
        vmem, any_ = pl.BlockSpec(memory_space=pltpu.VMEM), pl.BlockSpec(memory_space=pl.ANY)
        shapes = (
            jax.ShapeDtypeStruct(whole, jnp.float32),
            jax.ShapeDtypeStruct((1, count), jnp.float32),
            jax.ShapeDtypeStruct(whole, jnp.float32),
        )
        parts = pl.pallas_call(
            functools.partial(kernel, (levels, rows, cols, count, n_tm, n_patch)),
            out_shape=shapes,
            in_specs=[vmem] * 4 + [any_] * 6,
            out_specs=(any_, vmem, any_),
            scratch_shapes=scratch,
            compiler_params=pltpu.CompilerParams(
                collective_id=0, has_side_effects=True, vmem_limit_bytes=60 * 1024 * 1024
            ),
        )(
            obsm, obsv, cell, perm, mult.reshape(whole), inc.reshape(whole), err.reshape(whole),
            div.reshape(whole), bih.reshape(whole), w.reshape(2 * levels, count),
        )
        model, obs, state = pl.pallas_call(
            hand_over,
            out_shape=shapes,
            in_specs=[any_] * 3,
            out_specs=(any_,) * 3,
            scratch_shapes=[f32(whole), f32((1, count)), f32(whole), pltpu.SemaphoreType.DMA((4 * CHUNKS + 2,))],
            compiler_params=pltpu.CompilerParams(vmem_limit_bytes=60 * 1024 * 1024),
        )(*parts)
        return model[None], obs, state[None]

    field = P("tm", None, None, "patch", None)
    per_obs = P("tm", "patch")
    return jax.shard_map(
        per_device,
        mesh=mesh,
        in_specs=(
            field, per_obs, field, field, per_obs, field, field,
            P("tm", None, None, "patch"), per_obs, P("patch", None),
        ),
        out_specs=(field, per_obs, field),
        check_vma=False,
    )
```

time: 55 us -> 41.5 us (0.75)
  the two profiles are of different devices: /device:TPU:56 before, /device:TPU:71 now
where the time goes in v1:
time: 41.5 us; the launch traced here: 41.3 us
  Pallas kernels  40.7 us (98%)
  between operations  0.64 us (2%)
    pallas_call x1, Pallas kernels, per_device(): pl.pallas_call(functools.partial(kernel, (levels, rows, cols, count, n_tm...  38.5 us
    pallas_call x1, Pallas kernels, per_device(): pl.pallas_call(hand_over, out_shape=shapes, in_specs=[any_] * 3, out_spec...  2.11 us

profile of v1, /device:TPU:71, one launch (start us, length us, event | category | flops | bytes accessed | tf_op | source)
XLA Modules:
  0.0 41.3 jit_solution(2110758823080005668)
XLA Ops:
  0.6 38.5 %shard_map.121 = (f32[2,16,32,128]{3,2,1,0:T(8,128)}, f32[1,1024]{1,0:T(1,128)}, f32[2,16,32,128]{3,2,1,0:T(8,128)}) custom-call(f32[1,1024]{1,0:T(1,128)} %obsm.1, f32[1,1024]{1,0:T(1,128)} %obsv.1, s32[1,1024]{1,0:T(1,128)} %cell.1, s32[1,128]{1,0:T(1,128)} %perm.1, f32[2,16,32,128]{3,2,1,0:T(8,128)} %bitcast.8, f32[2,16,32,128]{3,2,1,0:T(8,128)} %bitcast.9, ...), custom_call_target="tpu_custom_call" | custom-call | tf_op jit(solution)/shard_map/pallas_call | solution.py:498
  39.2 2.1 %shard_map.122 = (f32[2,16,32,128]{3,2,1,0:T(8,128)}, f32[1,1024]{1,0:T(1,128)}, f32[2,16,32,128]{3,2,1,0:T(8,128)}) custom-call(f32[2,16,32,128]{3,2,1,0:T(8,128)} %get-tuple-element.9.model_i, f32[1,1024]{1,0:T(1,128)} %get-tuple-element.10.obs_i, f32[2,16,32,128]{3,2,1,0:T(8,128)} %get-tuple-element.11.state_i), custom_call_target="tpu_custom_call" | custom-call | tf_op jit(solution)/shard_map/pallas_call | solution.py:511

commit v2 on v1

--- a/solution.py
+++ b/solution.py
@@ -94,8 +94,8 @@
 def kernel(
     sizes,
     obsm, obsv, cell, perm, mult_h, inc_h, err_h, div_h, bih_h, w_h,
-    model_h, obs_o, state_h,
-    model, state, mult, inc, err, div, bih, w, prev,
+    model, obs_o, state,
+    mult, inc, err, div, bih, w, prev,
     adj_in, adj_ed, bwd_in, bwd_ed,
     up_s, down_s, inc_up_s, inc_down_s, low_r, high_r, prev_low, prev_high, perm_s, perm_r,
     a_hi, a_lo, wide, hot,
@@ -106,10 +106,9 @@
     k, p = lax.axis_index("tm"), lax.axis_index("patch")
     k_next, k_prev = lax.rem(k + 1, n_tm), lax.rem(k + n_tm - 1, n_tm)
     p_next, p_prev = lax.rem(p + 1, n_patch), lax.rem(p + n_patch - 1, n_patch)
-    even = lax.rem(p, 2) == 0
-    odd = lax.rem(p, 2) == 1
-    first = lax.rem(p, 4) == 0
-    later = lax.rem(p, 4) != 0
+    has_next, has_prev = k < n_tm - 1, k > 0
+    quad = lax.rem(p, 4)
+    early, late = quad < 2, quad >= 2
 
     loads = [
         pltpu.make_async_copy(src, dst, load_sem.at[i])
@@ -130,7 +129,7 @@
         pl.semaphore_signal(note_sem.at[index], inc=1, device_id=peer, device_id_type=MESH)
 
     RIM_UP, RIM_DOWN, BACK_IN, BACK_ED, BULK, INC_UP, INC_DOWN, PERM = (i * CHUNKS for i in range(8))
-    FROM_ABOVE, FROM_BELOW, BESIDE_ABOVE, BESIDE_BELOW, GO_ABOVE, GO_BELOW = range(6)
+    FROM_ABOVE, FROM_BELOW, BESIDE_ABOVE, BESIDE_BELOW = range(4)
 
     def rim_up(c):
         return remote(RIM_UP + c, up_s.at[c], low_r.at[c], (k, p_next))
@@ -163,23 +162,46 @@
             for c in range(CHUNKS):
                 copy(c).start()
 
+    def start_next(*copies):
+        @pl.when(has_next)
+        def _():
+            start_all(*copies)
+
     barrier = pltpu.get_barrier_semaphore()
-
-    @pl.when(even)
-    def _():
-        for peer in ((k_prev, p), (k_next, p), (k, p_prev), (k, p_next)):
-            pl.semaphore_signal(barrier, inc=1, device_id=peer, device_id_type=MESH)
-
-    pl.semaphore_wait(barrier, 2)
-
-    @pl.when(odd)
+    for peer in ((k_prev, p), (k_next, p)):
+        pl.semaphore_signal(barrier, inc=1, device_id=peer, device_id_type=MESH)
+
+    @pl.when(quad != 3)
+    def _():
+        pl.semaphore_signal(barrier, inc=1, device_id=(k, p_next), device_id_type=MESH)
+
+    @pl.when(quad == 0)
+    def _():
+        pl.semaphore_signal(barrier, inc=1, device_id=(k, p_prev), device_id_type=MESH)
+
+    pl.semaphore_wait(barrier, jnp.where(quad == 0, 2, jnp.where(quad == 3, 4, 3)))
+
+    def send_inc_up():
+        pl.semaphore_wait(note_sem.at[BESIDE_ABOVE], 1)
+        start_next(inc_up)
+
+    def send_inc_down():
+        pl.semaphore_wait(note_sem.at[BESIDE_BELOW], 1)
+        start_next(inc_down)
+
+    @pl.when(quad != 0)
     def _():
         note(FROM_ABOVE, (k, p_prev))
+        note(BESIDE_BELOW, (k_prev, p))
+
+    @pl.when(quad == 3)
+    def _():
         note(FROM_BELOW, (k, p_next))
-
-    @pl.when(even)
-    def _():
-        start_all(bulk)
+        note(BESIDE_ABOVE, (k_prev, p))
+
+    @pl.when(early)
+    def _():
+        start_next(bulk)
 
     st = Stencil(cols)
     perm_s[...] = jnp.broadcast_to(perm[...], perm_s.shape)
@@ -207,10 +229,22 @@
         send_perm.start()
         start_all(rim_down)
 
-    @pl.when(odd)
-    def _():
+    def meet_above():
+        pl.semaphore_wait(note_sem.at[FROM_ABOVE], 1)
         send_up()
+        note(BESIDE_ABOVE, (k_prev, p))
+
+    @pl.when(quad != 0)
+    def _():
         send_down()
+
+    @pl.when(quad == 3)
+    def _():
+        send_up()
+
+    @pl.when(quad == 2)
+    def _():
+        meet_above()
 
     loads[3].wait()
 
@@ -221,6 +255,14 @@
         return 0
 
     lax.fori_loop(0, CHUNKS, pack_inc, 0)
+
+    @pl.when(quad != 0)
+    def _():
+        send_inc_down()
+
+    @pl.when(late)
+    def _():
+        send_inc_up()
 
     def inner(field, lev):
         return [field[lev, HALO + 8 * i : HALO + 8 * (i + 1), :] for i in range(rows // 8 - 1)]
@@ -235,42 +277,25 @@
                 for i in range(rows // 8 - 2):
                     adj_in[var, lev, 8 * i : 8 * (i + 1), :] = st.shift(f[i], f[i + 1])
 
-        @pl.when(even)
+        @pl.when(early & has_prev)
         def _():
             back_in(c).start()
 
         return 0
 
-    @pl.when(first)
-    def _():
-        lax.fori_loop(0, CHUNKS, adjoint_inside, 0)
-
-    @pl.when(even)
-    def _():
-        pl.semaphore_wait(note_sem.at[FROM_ABOVE], 1)
-        send_up()
-        note(BESIDE_ABOVE, (k_prev, p))
-        note(BESIDE_ABOVE, (k_next, p))
-        pl.semaphore_wait(note_sem.at[FROM_BELOW], 1)
-        send_down()
-        note(BESIDE_BELOW, (k_prev, p))
-        note(BESIDE_BELOW, (k_next, p))
-        pl.semaphore_wait(note_sem.at[BESIDE_ABOVE], 2)
-        note(GO_BELOW, (k, p_next))
-        start_all(inc_up)
-        pl.semaphore_wait(note_sem.at[BESIDE_BELOW], 2)
-        note(GO_ABOVE, (k, p_prev))
-        start_all(inc_down)
-
-    @pl.when(odd)
-    def _():
-        pl.semaphore_wait(note_sem.at[GO_BELOW], 1)
-        pl.semaphore_wait(note_sem.at[GO_ABOVE], 1)
-        start_all(inc_up, inc_down)
-
-    @pl.when(later)
-    def _():
-        lax.fori_loop(0, CHUNKS, adjoint_inside, 0)
+    lax.fori_loop(0, CHUNKS, adjoint_inside, 0)
+
+    @pl.when(early)
+    def _():
+        meet_above()
+
+    @pl.when(quad == 1)
+    def _():
+        send_inc_up()
+
+    @pl.when(late)
+    def _():
+        start_next(bulk)
 
     half = rows // 2
     cells = cell[...]
@@ -311,17 +336,24 @@
     state[:, :, :half, :] = mult[:, :, :half, :] + spread[..., :cols]
     state[:, :, half:, :] = mult[:, :, half:, :] + spread[..., cols:]
 
-    @pl.when(odd)
-    def _():
-        start_all(bulk)
+    @pl.when(quad == 0)
+    def _():
+        send_inc_up()
+        pl.semaphore_wait(note_sem.at[FROM_BELOW], 1)
+        send_down()
+        note(BESIDE_BELOW, (k_prev, p))
+        send_inc_down()
 
     def keep(var, lev, at, f):
         span = slice(at, at + 8)
         rest = err[var, lev, span, :] * mult[var, lev, span, :] + inc[var, lev, span, :]
-        model[var, lev, span, :] = rest - jnp.where(k == 0, 0.0, f)
+        model[var, lev, span, :] = rest - jnp.where(has_prev, f, 0.0)
 
     def forward_inside(c, _):
-        bulk(c).wait_recv()
+        @pl.when(has_prev)
+        def _():
+            bulk(c).wait_recv()
+
         for g in range(per):
             lev = c * per + g
             u, v = inner(prev.at[0], lev), inner(prev.at[1], lev)
@@ -335,7 +367,7 @@
     def all_forward_inside():
         lax.fori_loop(0, CHUNKS, forward_inside, 0)
 
-    @pl.when(even)
+    @pl.when(early)
     def _():
         all_forward_inside()
 
@@ -377,16 +409,19 @@
                 adj_ed[var, lev, :8, :] = st.shift(f[0], f[1])
                 adj_ed[var, lev, 8:, :] = st.shift(f[2], f[3])
 
-        @pl.when(odd)
+        @pl.when(late & has_prev)
         def _():
             back_in(c).start()
 
-        back_ed(c).start()
+        @pl.when(has_prev)
+        def _():
+            back_ed(c).start()
+
         return 0
 
     lax.fori_loop(0, CHUNKS, adjoint_border, 0)
 
-    @pl.when(odd)
+    @pl.when(late)
     def _():
         all_forward_inside()
 
@@ -399,8 +434,11 @@
         return pltpu.make_async_copy(state.at[:, span], state_h.at[:, span], store_sem.at[CHUNKS + c])
 
     def forward_border(c, _):
-        inc_up(c).wait_recv()
-        inc_down(c).wait_recv()
+        @pl.when(has_prev)
+        def _():
+            inc_up(c).wait_recv()
+            inc_down(c).wait_recv()
+
         for g in range(per):
             lev = c * per + g
             u, v = (border(prev.at[var], prev_high[c, var, g], prev_low[c, var, g], lev) for var in range(2))
@@ -409,52 +447,54 @@
             for var, f in ((0, u), (1, v)):
                 keep(var, lev, rows - 8, st.shift(f[0], f[1]))
                 keep(var, lev, 0, st.shift(f[2], f[3]))
-        model_out(c).start()
         return 0
 
     lax.fori_loop(0, CHUNKS, forward_border, 0)
-    is_last = k == n_tm - 1
 
     def finish(c, _):
         span = pl.ds(c * per, per)
-        back_in(c).wait_recv()
+
+        @pl.when(has_next)
+        def _():
+            back_in(c).wait_recv()
+            back_ed(c).wait_recv()
+
         inside = pl.ds(8, rows - 16)
-        state[:, span, inside, :] = state[:, span, inside, :] - jnp.where(is_last, 0.0, bwd_in[:, span])
-        back_ed(c).wait_recv()
+        state[:, span, inside, :] = state[:, span, inside, :] - jnp.where(has_next, bwd_in[:, span], 0.0)
         for at, place in ((rows - 8, 0), (0, 8)):
             part = bwd_ed[:, span, place : place + 8, :]
-            state[:, span, at : at + 8, :] = state[:, span, at : at + 8, :] - jnp.where(is_last, 0.0, part)
-        state_out(c).start()
+            state[:, span, at : at + 8, :] = state[:, span, at : at + 8, :] - jnp.where(has_next, part, 0.0)
         return 0
 
     lax.fori_loop(0, CHUNKS, finish, 0)
 
     def sent(c, _):
-        for copy in (rim_up(c), rim_down(c), back_in(c), back_ed(c), bulk(c), inc_up(c), inc_down(c)):
-            copy.wait_send()
-        model_out(c).wait()
-        state_out(c).wait()
+        rim_up(c).wait_send()
+        rim_down(c).wait_send()
+
+        @pl.when(has_prev)
+        def _():
+            back_in(c).wait_send()
+            back_ed(c).wait_send()
+
+        @pl.when(has_next)
+        def _():
+            bulk(c).wait_send()
+            inc_up(c).wait_send()
+            inc_down(c).wait_send()
+
         return 0
 
     lax.fori_loop(0, CHUNKS, sent, 0)
     send_perm.wait_send()
 
 
-def hand_over(model_i, obs_i, state_i, model_o, obs_o, state_o, model, obs, state, sems):
-    per = model.shape[1] // CHUNKS
-    routes = [(obs_i, obs, obs_o)]
-    for c in range(CHUNKS):
-        span = pl.ds(c * per, per)
-        routes.append((model_i.at[:, span], model.at[:, span], model_o.at[:, span]))
-        routes.append((state_i.at[:, span], state.at[:, span], state_o.at[:, span]))
-    ins = [pltpu.make_async_copy(a, b, sems.at[i]) for i, (a, b, _) in enumerate(routes)]
-    outs = [pltpu.make_async_copy(b, c, sems.at[len(routes) + i]) for i, (_, b, c) in enumerate(routes)]
-    for copy in ins:
+def hand_over(*refs):
+    sems = refs[-1]
+    copies = [pltpu.make_async_copy(refs[i], refs[3 + i], sems.at[i]) for i in range(3)]
+    for copy in copies:
         copy.start()
-    for came, goes in zip(ins, outs):
-        came.wait()
-        goes.start()
-    for copy in outs:
+    for copy in copies:
         copy.wait()
 
 
@@ -469,7 +509,7 @@
         rim = (CHUNKS, 2, per, HALO, cols)
         rims = (CHUNKS, 5, per, HALO, cols)
         f32 = functools.partial(pltpu.VMEM, dtype=jnp.float32)
-        scratch = [f32(whole)] * 7 + [f32((2 * levels, count)), f32(whole)]
+        scratch = [f32(whole)] * 5 + [f32((2 * levels, count)), f32(whole)]
         scratch += [f32((2, levels, rows - 16, cols)), f32((2, levels, 16, cols))] * 2
         scratch += [f32(rims)] * 2 + [f32(rim)] * 2
         scratch += [f32(rims)] * 2 + [f32(rim)] * 2
@@ -487,7 +527,7 @@
             pltpu.SemaphoreType.DMA((copies,)),
             pltpu.SemaphoreType.DMA((copies,)),
             pltpu.SemaphoreType.DMA((2 * CHUNKS,)),
-            pltpu.SemaphoreType.REGULAR((6,)),
+            pltpu.SemaphoreType.REGULAR((4,)),
         ]
         vmem, any_ = pl.BlockSpec(memory_space=pltpu.VMEM), pl.BlockSpec(memory_space=pl.ANY)
         shapes = (
@@ -497,12 +537,12 @@
         )
         parts = pl.pallas_call(
             functools.partial(kernel, (levels, rows, cols, count, n_tm, n_patch)),
-            out_shape=shapes,
+            out_shape=tuple(pltpu.VMEM(x.shape, x.dtype) for x in shapes),
             in_specs=[vmem] * 4 + [any_] * 6,
-            out_specs=(any_, vmem, any_),
+            out_specs=(vmem, vmem, vmem),
             scratch_shapes=scratch,
             compiler_params=pltpu.CompilerParams(
-                collective_id=0, has_side_effects=True, vmem_limit_bytes=60 * 1024 * 1024
+                collective_id=0, has_side_effects=True, vmem_limit_bytes=62914560
             ),
         )(
             obsm, obsv, cell, perm, mult.reshape(whole), inc.reshape(whole), err.reshape(whole),
@@ -511,10 +551,10 @@
         model, obs, state = pl.pallas_call(
             hand_over,
             out_shape=shapes,
-            in_specs=[any_] * 3,
+            in_specs=[vmem] * 3,
             out_specs=(any_,) * 3,
-            scratch_shapes=[f32(whole), f32((1, count)), f32(whole), pltpu.SemaphoreType.DMA((4 * CHUNKS + 2,))],
-            compiler_params=pltpu.CompilerParams(vmem_limit_bytes=60 * 1024 * 1024),
+            scratch_shapes=[pltpu.SemaphoreType.DMA((3,))],
+            compiler_params=pltpu.CompilerParams(vmem_limit_bytes=16777216),
         )(*parts)
         return model[None], obs, state[None]
 

time: 41.5 us -> 34.3 us (0.83)
  the two profiles are of different devices: /device:TPU:71 before, /device:TPU:42 now
where the time goes in v2:
time: 34.3 us; the launch traced here: 34.1 us
  Pallas kernels  33.5 us (98%)
  between operations  0.64 us (2%)
    pallas_call x1, Pallas kernels, per_device(): pl.pallas_call(functools.partial(kernel, (levels, rows, cols, count, n_tm...  32.5 us
    pallas_call x1, Pallas kernels, per_device(): pl.pallas_call(hand_over, out_shape=shapes, in_specs=[vmem] * 3, out_spec...  1 us

profile of v2, /device:TPU:42, one launch (start us, length us, event | category | flops | bytes accessed | tf_op | source)
XLA Modules:
  0.0 34.1 jit_solution(9863575942757139296)
XLA Ops:
  0.6 32.5 %shard_map.121 = (f32[2,16,32,128]{3,2,1,0:T(8,128)S(1)}, f32[1,1024]{1,0:T(1,128)S(1)}, f32[2,16,32,128]{3,2,1,0:T(8,128)S(1)}) custom-call(f32[1,1024]{1,0:T(1,128)} %obsm.1, f32[1,1024]{1,0:T(1,128)} %obsv.1, s32[1,1024]{1,0:T(1,128)} %cell.1, s32[1,128]{1,0:T(1,128)} %perm.1, f32[2,16,32,128]{3,2,1,0:T(8,128)} %bitcast.8, f32[2,16,32,128]{3,2,1,0:T(8,128)} %bitcast.9, ...), custom_call_target="tpu_custom_call" | custom-call | tf_op jit(solution)/shard_map/pallas_call | solution.py:538
  33.1 1.0 %shard_map.122 = (f32[2,16,32,128]{3,2,1,0:T(8,128)}, f32[1,1024]{1,0:T(1,128)}, f32[2,16,32,128]{3,2,1,0:T(8,128)}) custom-call(f32[2,16,32,128]{3,2,1,0:T(8,128)S(1)} %get-tuple-element.9.refs_0_, f32[1,1024]{1,0:T(1,128)S(1)} %get-tuple-element.10.refs_1_, f32[2,16,32,128]{3,2,1,0:T(8,128)S(1)} %get-tuple-element.11.refs_2_), custom_call_target="tpu_custom_call" | custom-call | tf_op jit(solution)/shard_map/pallas_call | solution.py:551

commit v3 on v2

--- a/solution.py
+++ b/solution.py
@@ -8,7 +8,6 @@
 from jax.sharding import PartitionSpec as P
 
 MESH = pl.DeviceIdType.MESH
-HALO = 4
 CHUNKS = 4
 
 
@@ -43,7 +42,8 @@
         self.lane = lax.broadcasted_iota(jnp.int32, (8, cols), 1)
         self.first, self.last = self.lane == 0, self.lane == cols - 1
         self.top, self.bottom = self.row == 7, self.row == 0
-        self.low_side, self.high_side = self.row == 3, self.row == 4
+        self.below_edge = (self.row == 5, self.row == 1)
+        self.above_edge = (self.row == 6, self.row == 2)
 
     def up(self, tiles):
         r = [pltpu.roll(t, 7, 0) for t in tiles]
@@ -55,10 +55,10 @@
 
     def rows_around(self, tiles, seams):
         above, below = list(tiles), list(tiles)
-        for i, index in seams:
+        for i, index in enumerate(seams):
             crossed = lane_take(tiles[i], index)
-            above[i] = jnp.where(self.high_side, crossed, tiles[i])
-            below[i] = jnp.where(self.low_side, crossed, tiles[i])
+            above[i] = jnp.where(self.above_edge[i], crossed, tiles[i])
+            below[i] = jnp.where(self.below_edge[i], crossed, tiles[i])
         return self.up(above), self.down(below)
 
     def right(self, tiles):
@@ -87,8 +87,14 @@
         ]
         return out_u, out_v
 
-    def shift(self, x, y):
-        return jnp.where(self.row < 4, pltpu.roll(x, 4, 0), pltpu.roll(y, 4, 0))
+    def turn(self, x, by):
+        return x if by % 8 == 0 else pltpu.roll(x, by % 8, 0)
+
+    def ends(self, first, last, high, low):
+        return [
+            jnp.where(self.row < 6, self.turn(last, 6), high),
+            jnp.where(self.row < 2, low, self.turn(first, 2)),
+        ]
 
 
 def kernel(
@@ -96,8 +102,8 @@
     obsm, obsv, cell, perm, mult_h, inc_h, err_h, div_h, bih_h, w_h,
     model, obs_o, state,
     mult, inc, err, div, bih, w, prev,
-    adj_in, adj_ed, bwd_in, bwd_ed,
-    up_s, down_s, inc_up_s, inc_down_s, low_r, high_r, prev_low, prev_high, perm_s, perm_r,
+    adj_in, adj_ed, bwd_in, bwd_ed, mid_a, mid_f,
+    up_s, down_s, low_r, high_r, four_s, four_r, perm_s, perm_r,
     a_hi, a_lo, wide, hot,
     load_sem, send_sem, recv_sem, store_sem, note_sem,
 ):
@@ -116,7 +122,7 @@
             ((mult_h, mult), (div_h, div), (bih_h, bih), (inc_h, inc), (w_h, w), (err_h, err))
         )
     ]
-    for load in loads:
+    for load in loads[:3]:
         load.start()
 
     def remote(index, src, dst, peer):
@@ -128,7 +134,10 @@
     def note(index, peer):
         pl.semaphore_signal(note_sem.at[index], inc=1, device_id=peer, device_id_type=MESH)
 
-    RIM_UP, RIM_DOWN, BACK_IN, BACK_ED, BULK, INC_UP, INC_DOWN, PERM = (i * CHUNKS for i in range(8))
+    RIM_UP, RIM_DOWN, BACK_IN, BACK_ED, BULK, INC_UP, INC_DOWN, ADJ_UP, ADJ_DOWN, FWD_UP, FWD_DOWN, PERM = (
+        i * CHUNKS for i in range(12)
+    )
+    BULK_ENDS = PERM + 1
     FROM_ABOVE, FROM_BELOW, BESIDE_ABOVE, BESIDE_BELOW = range(4)
 
     def rim_up(c):
@@ -148,14 +157,30 @@
     send_perm = remote(PERM, perm_s, perm_r, (k, p_prev))
 
     def bulk(c):
-        span = pl.ds(c * per, per)
-        return remote(BULK + c, inc_h.at[:, span], prev.at[:, span], (k_next, p))
+        part = (slice(None), pl.ds(c * per, per), pl.ds(8, rows - 16))
+        return remote(BULK + c, inc_h.at[part], prev.at[part], (k_next, p))
+
+    def bulk_end(i):
+        part = (slice(None), slice(None), pl.ds(i * (rows - 8), 8))
+        return remote(BULK_ENDS + i, inc_h.at[part], prev.at[part], (k_next, p))
 
     def inc_up(c):
-        return remote(INC_UP + c, inc_up_s.at[c], prev_low.at[c], (k_next, p_next))
+        return remote(INC_UP + c, four_s.at[0, c], four_r.at[0, c], (k_next, p_next))
 
     def inc_down(c):
-        return remote(INC_DOWN + c, inc_down_s.at[c], prev_high.at[c], (k_next, p_prev))
+        return remote(INC_DOWN + c, four_s.at[1, c], four_r.at[1, c], (k_next, p_prev))
+
+    def adj_up(c):
+        return remote(ADJ_UP + c, four_s.at[2, c], four_r.at[2, c], (k, p_next))
+
+    def adj_down(c):
+        return remote(ADJ_DOWN + c, four_s.at[3, c], four_r.at[3, c], (k, p_prev))
+
+    def fwd_up(c):
+        return remote(FWD_UP + c, four_s.at[4, c], four_r.at[4, c], (k, p_next))
+
+    def fwd_down(c):
+        return remote(FWD_DOWN + c, four_s.at[5, c], four_r.at[5, c], (k, p_prev))
 
     def start_all(*copies):
         for copy in copies:
@@ -199,6 +224,11 @@
         note(FROM_BELOW, (k, p_next))
         note(BESIDE_ABOVE, (k_prev, p))
 
+    @pl.when(has_next)
+    def _():
+        bulk_end(0).start()
+        bulk_end(1).start()
+
     @pl.when(early)
     def _():
         start_next(bulk)
@@ -207,17 +237,18 @@
     perm_s[...] = jnp.broadcast_to(perm[...], perm_s.shape)
     for load in loads[:3]:
         load.wait()
+    for load in loads[3:]:
+        load.start()
 
     def pack(c, _):
         span = pl.ds(c * per, per)
         for var in range(2):
-            up_s[c, var] = mult[var, span, rows - HALO :, :]
-            down_s[c, var] = mult[var, span, :HALO, :]
-        for i, coef in enumerate((div.at[0], div.at[1], bih.at[0])):
-            up_s[c, 2 + i, :, 1:, :] = coef[span, rows - 3 :, :]
-            up_s[c, 2 + i, :, :1, :] = bih[1, span, rows - 3 + i : rows - 2 + i, :]
-            down_s[c, 2 + i, :, :3, :] = coef[span, :3, :]
-            down_s[c, 2 + i, :, 3:, :] = bih[1, span, i : i + 1, :]
+            up_s[c, :, 2 * var : 2 * var + 2, :] = mult[var, span, rows - 2 :, :]
+            down_s[c, :, 2 * var : 2 * var + 2, :] = mult[var, span, :2, :]
+            up_s[c, :, 4 + var : 5 + var, :] = div[var, span, rows - 1 :, :]
+            up_s[c, :, 6 + var : 7 + var, :] = bih[var, span, rows - 1 :, :]
+            down_s[c, :, 4 + var : 5 + var, :] = bih[var, span, :1, :]
+            down_s[c, :, 6 + var : 7 + var, :] = bih[var, span, :1, :]
         return 0
 
     lax.fori_loop(0, CHUNKS, pack, 0)
@@ -249,9 +280,11 @@
     loads[3].wait()
 
     def pack_inc(c, _):
-        span = pl.ds(c * per, per)
-        inc_up_s[c] = inc[:, span, rows - HALO :, :]
-        inc_down_s[c] = inc[:, span, :HALO, :]
+        for g in range(per):
+            for var in range(2):
+                at = 4 * (g % 2) + 2 * var
+                four_s[0, c, g // 2, at : at + 2, :] = inc[var, c * per + g, rows - 2 :, :]
+                four_s[1, c, g // 2, at : at + 2, :] = inc[var, c * per + g, :2, :]
         return 0
 
     lax.fori_loop(0, CHUNKS, pack_inc, 0)
@@ -264,18 +297,29 @@
     def _():
         send_inc_up()
 
-    def inner(field, lev):
-        return [field[lev, HALO + 8 * i : HALO + 8 * (i + 1), :] for i in range(rows // 8 - 1)]
+    def tiles(field, lev):
+        return [field[lev, 8 * i : 8 * (i + 1), :] for i in range(rows // 8)]
+
+    def inside(lev, field, mid, order):
+        u, v = tiles(field.at[0], lev), tiles(field.at[1], lev)
+        for at, s in enumerate(order):
+            u, v = st.step(u, v, tiles(div.at[s], lev), tiles(bih.at[s], lev), ())
+            if at == 0:
+                for var, f in ((0, u), (1, v)):
+                    mid[var, lev, 2:8, :] = f[0][2:]
+                    for i in range(1, rows // 8 - 1):
+                        mid[var, lev, 8 * i : 8 * (i + 1), :] = f[i]
+                    mid[var, lev, rows - 8 : rows - 2, :] = f[-1][:6]
+        return u, v
 
     def adjoint_inside(c, _):
         for g in range(per):
             lev = c * per + g
-            u, v = inner(mult.at[0], lev), inner(mult.at[1], lev)
-            for s in (1, 0):
-                u, v = st.step(u, v, inner(div.at[s], lev), inner(bih.at[s], lev), ())
-            for var, f in ((0, u), (1, v)):
-                for i in range(rows // 8 - 2):
-                    adj_in[var, lev, 8 * i : 8 * (i + 1), :] = st.shift(f[i], f[i + 1])
+            for var, f in enumerate(inside(lev, mult, mid_a, (1, 0))):
+                adj_in[var, lev, :4, :] = f[0][4:]
+                for i in range(1, rows // 8 - 1):
+                    adj_in[var, lev, 8 * i - 4 : 8 * i + 4, :] = f[i]
+                adj_in[var, lev, rows - 12 :, :] = f[-1][:4]
 
         @pl.when(early & has_prev)
         def _():
@@ -297,44 +341,50 @@
     def _():
         start_next(bulk)
 
-    half = rows // 2
-    cells = cell[...]
-    row = cells // cols
-    within = (row // half) * cols + cells % cols
-    group = row % half
-    hot[...] = (
-        lax.broadcasted_iota(jnp.int32, (2 * cols, count), 0) == jnp.broadcast_to(within, (2 * cols, count))
-    ).astype(jnp.float32).astype(jnp.bfloat16)
-    mask = lax.broadcasted_iota(jnp.int32, (half, count), 0) == jnp.broadcast_to(group, (half, count))
-    loads[4].wait()
-    loads[5].wait()
-    times = obsm[...]
-    for var in range(2):
-        for lev in range(levels):
-            at = (var * levels + lev) * half
-            weight = w[var * levels + lev : var * levels + lev + 1, :]
-            hi, lo = split(jnp.where(mask, jnp.broadcast_to(weight * times, mask.shape), 0.0))
-            a_hi[at : at + half] = hi
-            a_lo[at : at + half] = lo
-            plane = inc[var, lev]
-            hi, lo = split(jnp.concatenate([plane[:half], plane[half:]], 1))
-            wide[at : at + half, : 2 * cols] = hi
-            wide[at : at + half, 2 * cols :] = lo
-    block = min(256, count)
-    for start in range(0, count, block):
-        part = hot[:, start : start + block]
-        found = dot_nn(wide[...], jnp.concatenate([part, part], 0))
-        found = found.reshape(2 * levels, half, block)
-        found = jnp.where(mask[None, :, start : start + block], found, 0.0)
-        found = jnp.sum(found.reshape(2 * levels, half // 8, 8, block), 1)
-        found = found * w[:, start : start + block][:, None, :]
-        found = jnp.sum(jnp.sum(found, 0), 0, keepdims=True)
-        span = pl.ds(start, block)
-        obs_o[:, span] = obsv[:, span] * obsm[:, span] + found
-    spread = dot_nt(a_hi[...], hot[...]) + dot_nt(a_lo[...], hot[...])
-    spread = spread.reshape(2, levels, half, 2 * cols)
-    state[:, :, :half, :] = mult[:, :, :half, :] + spread[..., :cols]
-    state[:, :, half:, :] = mult[:, :, half:, :] + spread[..., cols:]
+    for load in loads[4:]:
+        load.wait()
+
+    def observations():
+        half = rows // 2
+        cells = cell[...]
+        row = cells // cols
+        within = (row // half) * cols + cells % cols
+        group = row % half
+        hot[...] = (
+            lax.broadcasted_iota(jnp.int32, (2 * cols, count), 0) == jnp.broadcast_to(within, (2 * cols, count))
+        ).astype(jnp.float32).astype(jnp.bfloat16)
+        mask = lax.broadcasted_iota(jnp.int32, (half, count), 0) == jnp.broadcast_to(group, (half, count))
+        times = obsm[...]
+        for var in range(2):
+            for lev in range(levels):
+                at = (var * levels + lev) * half
+                weight = w[var * levels + lev : var * levels + lev + 1, :]
+                hi, lo = split(jnp.where(mask, jnp.broadcast_to(weight * times, mask.shape), 0.0))
+                a_hi[at : at + half] = hi
+                a_lo[at : at + half] = lo
+                plane = inc[var, lev]
+                hi, lo = split(jnp.concatenate([plane[:half], plane[half:]], 1))
+                wide[at : at + half, : 2 * cols] = hi
+                wide[at : at + half, 2 * cols :] = lo
+        block = min(256, count)
+        for start in range(0, count, block):
+            part = hot[:, start : start + block]
+            found = dot_nn(wide[...], jnp.concatenate([part, part], 0))
+            found = found.reshape(2 * levels, half, block)
+            found = jnp.where(mask[None, :, start : start + block], found, 0.0)
+            found = jnp.sum(found.reshape(2 * levels, half // 8, 8, block), 1)
+            found = found * w[:, start : start + block][:, None, :]
+            found = jnp.sum(jnp.sum(found, 0), 0, keepdims=True)
+            span = pl.ds(start, block)
+            obs_o[:, span] = obsv[:, span] * obsm[:, span] + found
+        spread = dot_nt(a_hi[...], hot[...]) + dot_nt(a_lo[...], hot[...])
+        spread = spread.reshape(2, levels, half, 2 * cols)
+        state[:, :, :half, :] = mult[:, :, :half, :] + spread[..., :cols]
+        state[:, :, half:, :] = mult[:, :, half:, :] + spread[..., cols:]
+
+    @pl.when(early)
+    def _():
+        observations()
 
     @pl.when(quad == 0)
     def _():
@@ -345,7 +395,7 @@
         send_inc_down()
 
     def keep(var, lev, at, f):
-        span = slice(at, at + 8)
+        span = slice(at, at + f.shape[0])
         rest = err[var, lev, span, :] * mult[var, lev, span, :] + inc[var, lev, span, :]
         model[var, lev, span, :] = rest - jnp.where(has_prev, f, 0.0)
 
@@ -356,100 +406,141 @@
 
         for g in range(per):
             lev = c * per + g
-            u, v = inner(prev.at[0], lev), inner(prev.at[1], lev)
-            for s in (0, 1):
-                u, v = st.step(u, v, inner(div.at[s], lev), inner(bih.at[s], lev), ())
-            for var, f in ((0, u), (1, v)):
-                for i in range(rows // 8 - 2):
-                    keep(var, lev, 8 * (i + 1), st.shift(f[i], f[i + 1]))
+            for var, f in enumerate(inside(lev, prev, mid_f, (0, 1))):
+                keep(var, lev, 4, f[0][4:])
+                for i in range(1, rows // 8 - 1):
+                    keep(var, lev, 8 * i, f[i])
+                keep(var, lev, rows - 8, f[-1][:4])
         return 0
 
     def all_forward_inside():
+        @pl.when(early & has_prev)
+        def _():
+            bulk_end(0).wait_recv()
+            bulk_end(1).wait_recv()
+
         lax.fori_loop(0, CHUNKS, forward_inside, 0)
 
     @pl.when(early)
     def _():
         all_forward_inside()
 
-    def border(field, high, low, lev):
+    def outer(field, lev):
+        return field[lev, :8, :], field[lev, rows - 8 :, :]
+
+    def border(field, lev, high, low, at):
         return [
-            field[lev, rows - 12 : rows - 4, :],
-            jnp.concatenate([field[lev, rows - 4 :, :], high], 0),
-            jnp.concatenate([low, field[lev, :4, :]], 0),
-            field[lev, 4:12, :],
+            st.ends(*outer(field.at[var], lev), st.turn(high, 6 - at - 2 * var), st.turn(low, -at - 2 * var))
+            for var in range(2)
         ]
 
-    def coefs(c, g, s):
+    def border_coefs(c, g, s):
         lev = c * per + g
-        a = border(div.at[s], high_r[c, 2 + s, g], low_r[c, 2 + s, g], lev)
-        if s == 0:
-            high, low = high_r[c, 4, g], low_r[c, 4, g]
-        else:
-            high = jnp.concatenate([high_r[c, 2 + min(i, 2), g, 3:, :] for i in range(4)], 0)
-            low = jnp.concatenate([low_r[c, 2 + max(i - 1, 0), g, :1, :] for i in range(4)], 0)
-        return a, border(bih.at[s], high, low, lev)
+        high, low = high_r[c, g], low_r[c, g]
+        a, b = outer(div.at[s], lev), outer(bih.at[s], lev)
+        return (
+            st.ends(*a, st.turn(a[1], 6), st.turn(low, 1 - (4 + s))),
+            st.ends(*b, st.turn(high, 6 - (4 + s)), st.turn(low, 1 - (6 + s))),
+        )
+
+    def first_step(c, g, field, high, low, at, s, mid, above_s, below_s):
+        lev = c * per + g
+        found = st.step(*border(field, lev, high, low, at), *border_coefs(c, g, s), seams)
+        for var, f in enumerate(found):
+            place = 4 * (g % 2) + 2 * var
+            mid[var, lev, rows - 2 :, :] = f[0][4:6]
+            mid[var, lev, :2, :] = f[1][2:4]
+            above_s[c, g // 2, place : place + 2, :] = f[0][4:6]
+            below_s[c, g // 2, place : place + 2, :] = f[1][2:4]
+
+    def second_step(c, g, mid, high, low, s):
+        lev = c * per + g
+        return st.step(*border(mid, lev, high, low, 4 * (g % 2)), *border_coefs(c, g, s), seams)
 
     send_perm.wait_recv()
     own, above = perm_s[...], perm_r[...]
 
-    def seam(low_index, high_index):
-        return jnp.where(st.low_side, low_index, jnp.where(st.high_side, high_index, st.lane))
-
-    seams = ((1, seam(above, inverse_rows(above))), (2, seam(own, inverse_rows(own))))
-
-    def adjoint_border(c, _):
+    def seam(i, perm_index):
+        crossing = jnp.where(st.above_edge[i], inverse_rows(perm_index), st.lane)
+        return jnp.where(st.below_edge[i], perm_index, crossing)
+
+    seams = (seam(0, above), seam(1, own))
+
+    def adjoint_first(c, _):
         rim_up(c).wait_recv()
         rim_down(c).wait_recv()
         for g in range(per):
-            lev = c * per + g
-            u, v = (border(mult.at[var], high_r[c, var, g], low_r[c, var, g], lev) for var in range(2))
-            for s in (1, 0):
-                u, v = st.step(u, v, *coefs(c, g, s), seams)
-            for var, f in ((0, u), (1, v)):
-                adj_ed[var, lev, :8, :] = st.shift(f[0], f[1])
-                adj_ed[var, lev, 8:, :] = st.shift(f[2], f[3])
+            first_step(c, g, mult, high_r[c, g], low_r[c, g], 0, 1, mid_a, four_s.at[2], four_s.at[3])
+        adj_up(c).start()
+        adj_down(c).start()
 
         @pl.when(late & has_prev)
         def _():
             back_in(c).start()
 
-        @pl.when(has_prev)
-        def _():
-            back_ed(c).start()
-
-        return 0
-
-    lax.fori_loop(0, CHUNKS, adjoint_border, 0)
-
-    @pl.when(late)
-    def _():
-        all_forward_inside()
-
-    def model_out(c):
-        span = pl.ds(c * per, per)
-        return pltpu.make_async_copy(model.at[:, span], model_h.at[:, span], store_sem.at[c])
-
-    def state_out(c):
-        span = pl.ds(c * per, per)
-        return pltpu.make_async_copy(state.at[:, span], state_h.at[:, span], store_sem.at[CHUNKS + c])
-
-    def forward_border(c, _):
+        return 0
+
+    lax.fori_loop(0, CHUNKS, adjoint_first, 0)
+
+    @pl.when(late & has_prev)
+    def _():
+        bulk_end(0).wait_recv()
+        bulk_end(1).wait_recv()
+
+    def forward_first(c, _):
         @pl.when(has_prev)
         def _():
             inc_up(c).wait_recv()
             inc_down(c).wait_recv()
-
+            for g in range(per):
+                high, low = four_r[1, c, g // 2], four_r[0, c, g // 2]
+                first_step(c, g, prev, high, low, 4 * (g % 2), 0, mid_f, four_s.at[4], four_s.at[5])
+            fwd_up(c).start()
+            fwd_down(c).start()
+
+        return 0
+
+    lax.fori_loop(0, CHUNKS, forward_first, 0)
+
+    @pl.when(late)
+    def _():
+        observations()
+
+
+    def adjoint_second(c, _):
+        adj_up(c).wait_recv()
+        adj_down(c).wait_recv()
         for g in range(per):
-            lev = c * per + g
-            u, v = (border(prev.at[var], prev_high[c, var, g], prev_low[c, var, g], lev) for var in range(2))
-            for s in (0, 1):
-                u, v = st.step(u, v, *coefs(c, g, s), seams)
-            for var, f in ((0, u), (1, v)):
-                keep(var, lev, rows - 8, st.shift(f[0], f[1]))
-                keep(var, lev, 0, st.shift(f[2], f[3]))
-        return 0
-
-    lax.fori_loop(0, CHUNKS, forward_border, 0)
+            found = second_step(c, g, mid_a, four_r[3, c, g // 2], four_r[2, c, g // 2], 0)
+            for var, f in enumerate(found):
+                adj_ed[var, c * per + g] = jnp.where(st.row < 4, st.turn(f[0], 6), st.turn(f[1], 2))
+
+        @pl.when(has_prev)
+        def _():
+            back_ed(c).start()
+
+        return 0
+
+    lax.fori_loop(0, CHUNKS, adjoint_second, 0)
+
+    @pl.when(late)
+    def _():
+        all_forward_inside()
+
+    def forward_second(c, _):
+        @pl.when(has_prev)
+        def _():
+            fwd_up(c).wait_recv()
+            fwd_down(c).wait_recv()
+
+        for g in range(per):
+            found = second_step(c, g, mid_f, four_r[5, c, g // 2], four_r[4, c, g // 2], 1)
+            for var, f in enumerate(found):
+                keep(var, c * per + g, rows - 4, f[0][2:6])
+                keep(var, c * per + g, 0, f[1][2:6])
+        return 0
+
+    lax.fori_loop(0, CHUNKS, forward_second, 0)
 
     def finish(c, _):
         span = pl.ds(c * per, per)
@@ -459,11 +550,13 @@
             back_in(c).wait_recv()
             back_ed(c).wait_recv()
 
-        inside = pl.ds(8, rows - 16)
-        state[:, span, inside, :] = state[:, span, inside, :] - jnp.where(has_next, bwd_in[:, span], 0.0)
-        for at, place in ((rows - 8, 0), (0, 8)):
-            part = bwd_ed[:, span, place : place + 8, :]
-            state[:, span, at : at + 8, :] = state[:, span, at : at + 8, :] - jnp.where(has_next, part, 0.0)
+        for at, part in (
+            (4, bwd_in[:, span]),
+            (rows - 4, bwd_ed[:, span, :4, :]),
+            (0, bwd_ed[:, span, 4:, :]),
+        ):
+            place = slice(at, at + part.shape[2])
+            state[:, span, place, :] = state[:, span, place, :] - jnp.where(has_next, part, 0.0)
         return 0
 
     lax.fori_loop(0, CHUNKS, finish, 0)
@@ -471,15 +564,24 @@
     def sent(c, _):
         rim_up(c).wait_send()
         rim_down(c).wait_send()
+        adj_up(c).wait_send()
+        adj_down(c).wait_send()
 
         @pl.when(has_prev)
         def _():
             back_in(c).wait_send()
             back_ed(c).wait_send()
+            fwd_up(c).wait_send()
+            fwd_down(c).wait_send()
 
         @pl.when(has_next)
         def _():
             bulk(c).wait_send()
+
+            @pl.when(c < 2)
+            def _():
+                bulk_end(c).wait_send()
+
             inc_up(c).wait_send()
             inc_down(c).wait_send()
 
@@ -506,13 +608,11 @@
         count = obsm.shape[1]
         per = levels // CHUNKS
         whole = (2, levels, rows, cols)
-        rim = (CHUNKS, 2, per, HALO, cols)
-        rims = (CHUNKS, 5, per, HALO, cols)
+        eight, four = (CHUNKS, per, 8, cols), (6, CHUNKS, per // 2, 8, cols)
         f32 = functools.partial(pltpu.VMEM, dtype=jnp.float32)
         scratch = [f32(whole)] * 5 + [f32((2 * levels, count)), f32(whole)]
-        scratch += [f32((2, levels, rows - 16, cols)), f32((2, levels, 16, cols))] * 2
-        scratch += [f32(rims)] * 2 + [f32(rim)] * 2
-        scratch += [f32(rims)] * 2 + [f32(rim)] * 2
+        scratch += [f32((2, levels, rows - 8, cols)), f32((2, levels, 8, cols))] * 2
+        scratch += [f32(whole)] * 2 + [f32(eight)] * 4 + [f32(four)] * 2
         scratch += [pltpu.VMEM((8, cols), jnp.int32)] * 2
         tall = 2 * levels * (rows // 2)
         scratch += [
@@ -521,7 +621,7 @@
             pltpu.VMEM((tall, 4 * cols), jnp.bfloat16),
             pltpu.VMEM((2 * cols, count), jnp.bfloat16),
         ]
-        copies = 7 * CHUNKS + 1
+        copies = 11 * CHUNKS + 3
         scratch += [
             pltpu.SemaphoreType.DMA((6,)),
             pltpu.SemaphoreType.DMA((copies,)),

time: 34.3 us -> 33.2 us (0.968)
  the two profiles are of different devices: /device:TPU:42 before, /device:TPU:5 now
where the time goes in v3:
time: 33.2 us; the launch traced here: 33 us
  Pallas kernels  32.3 us (97%)
  between operations  0.64 us (2%)
    pallas_call x1, Pallas kernels, per_device(): pl.pallas_call(functools.partial(kernel, (levels, rows, cols, count, n_tm...  31.3 us
    pallas_call x1, Pallas kernels, per_device(): pl.pallas_call(hand_over, out_shape=shapes, in_specs=[vmem] * 3, out_spec...  1 us

profile of v3, /device:TPU:5, one launch (start us, length us, event | category | flops | bytes accessed | tf_op | source)
XLA Modules:
  0.0 33.0 jit_solution(16703373657051831398)
XLA Ops:
  0.6 31.3 %shard_map.121 = (f32[2,16,32,128]{3,2,1,0:T(8,128)S(1)}, f32[1,1024]{1,0:T(1,128)S(1)}, f32[2,16,32,128]{3,2,1,0:T(8,128)S(1)}) custom-call(f32[1,1024]{1,0:T(1,128)} %obsm.1, f32[1,1024]{1,0:T(1,128)} %obsv.1, s32[1,1024]{1,0:T(1,128)} %cell.1, s32[1,128]{1,0:T(1,128)} %perm.1, f32[2,16,32,128]{3,2,1,0:T(8,128)} %bitcast.8, f32[2,16,32,128]{3,2,1,0:T(8,128)} %bitcast.9, ...), custom_call_target="tpu_custom_call" | custom-call | tf_op jit(solution)/shard_map/pallas_call | solution.py:638
  32.0 1.0 %shard_map.122 = (f32[2,16,32,128]{3,2,1,0:T(8,128)}, f32[1,1024]{1,0:T(1,128)}, f32[2,16,32,128]{3,2,1,0:T(8,128)}) custom-call(f32[2,16,32,128]{3,2,1,0:T(8,128)S(1)} %get-tuple-element.9.refs_0_, f32[1,1024]{1,0:T(1,128)S(1)} %get-tuple-element.10.refs_1_, f32[2,16,32,128]{3,2,1,0:T(8,128)S(1)} %get-tuple-element.11.refs_2_), custom_call_target="tpu_custom_call" | custom-call | tf_op jit(solution)/shard_map/pallas_call | solution.py:651

commit v4 on v3

--- a/solution.py
+++ b/solution.py
@@ -115,6 +115,7 @@
     has_next, has_prev = k < n_tm - 1, k > 0
     quad = lax.rem(p, 4)
     early, late = quad < 2, quad >= 2
+    inside_first, inside_last = quad == 0, quad != 0
 
     loads = [
         pltpu.make_async_copy(src, dst, load_sem.at[i])
@@ -265,13 +266,13 @@
         send_up()
         note(BESIDE_ABOVE, (k_prev, p))
 
+    @pl.when(quad == 3)
+    def _():
+        send_up()
+
     @pl.when(quad != 0)
     def _():
         send_down()
-
-    @pl.when(quad == 3)
-    def _():
-        send_up()
 
     @pl.when(quad == 2)
     def _():
@@ -289,13 +290,13 @@
 
     lax.fori_loop(0, CHUNKS, pack_inc, 0)
 
+    @pl.when(late)
+    def _():
+        send_inc_up()
+
     @pl.when(quad != 0)
     def _():
         send_inc_down()
-
-    @pl.when(late)
-    def _():
-        send_inc_up()
 
     def tiles(field, lev):
         return [field[lev, 8 * i : 8 * (i + 1), :] for i in range(rows // 8)]
@@ -321,7 +322,7 @@
                     adj_in[var, lev, 8 * i - 4 : 8 * i + 4, :] = f[i]
                 adj_in[var, lev, rows - 12 :, :] = f[-1][:4]
 
-        @pl.when(early & has_prev)
+        @pl.when((quad == 0) & has_prev)
         def _():
             back_in(c).start()
 
@@ -414,14 +415,14 @@
         return 0
 
     def all_forward_inside():
-        @pl.when(early & has_prev)
+        @pl.when(inside_first & has_prev)
         def _():
             bulk_end(0).wait_recv()
             bulk_end(1).wait_recv()
 
         lax.fori_loop(0, CHUNKS, forward_inside, 0)
 
-    @pl.when(early)
+    @pl.when(inside_first)
     def _():
         all_forward_inside()
 
@@ -474,7 +475,7 @@
         adj_up(c).start()
         adj_down(c).start()
 
-        @pl.when(late & has_prev)
+        @pl.when((quad != 0) & has_prev)
         def _():
             back_in(c).start()
 
@@ -482,7 +483,7 @@
 
     lax.fori_loop(0, CHUNKS, adjoint_first, 0)
 
-    @pl.when(late & has_prev)
+    @pl.when(inside_last & has_prev)
     def _():
         bulk_end(0).wait_recv()
         bulk_end(1).wait_recv()
@@ -523,7 +524,7 @@
 
     lax.fori_loop(0, CHUNKS, adjoint_second, 0)
 
-    @pl.when(late)
+    @pl.when(inside_last)
     def _():
         all_forward_inside()
 

time: 33.2 us -> 33.2 us (level)
  no operation moved by 1% of the time
where the time goes in v4:
time: 33.2 us; the launch traced here: 33 us
  Pallas kernels  32.4 us (98%)
  between operations  0.64 us (2%)
    pallas_call x1, Pallas kernels, per_device(): pl.pallas_call(functools.partial(kernel, (levels, rows, cols, count, n_tm...  31.4 us
    pallas_call x1, Pallas kernels, per_device(): pl.pallas_call(hand_over, out_shape=shapes, in_specs=[vmem] * 3, out_spec...  1 us

profile of v4, /device:TPU:5, one launch (start us, length us, event | category | flops | bytes accessed | tf_op | source)
XLA Modules:
  0.0 33.0 jit_solution(7481989576504337492)
XLA Ops:
  0.6 31.4 %shard_map.121 = (f32[2,16,32,128]{3,2,1,0:T(8,128)S(1)}, f32[1,1024]{1,0:T(1,128)S(1)}, f32[2,16,32,128]{3,2,1,0:T(8,128)S(1)}) custom-call(f32[1,1024]{1,0:T(1,128)} %obsm.1, f32[1,1024]{1,0:T(1,128)} %obsv.1, s32[1,1024]{1,0:T(1,128)} %cell.1, s32[1,128]{1,0:T(1,128)} %perm.1, f32[2,16,32,128]{3,2,1,0:T(8,128)} %bitcast.8, f32[2,16,32,128]{3,2,1,0:T(8,128)} %bitcast.9, ...), custom_call_target="tpu_custom_call" | custom-call | tf_op jit(solution)/shard_map/pallas_call | solution.py:639
  32.0 1.0 %shard_map.122 = (f32[2,16,32,128]{3,2,1,0:T(8,128)}, f32[1,1024]{1,0:T(1,128)}, f32[2,16,32,128]{3,2,1,0:T(8,128)}) custom-call(f32[2,16,32,128]{3,2,1,0:T(8,128)S(1)} %get-tuple-element.9.refs_0_, f32[1,1024]{1,0:T(1,128)S(1)} %get-tuple-element.10.refs_1_, f32[2,16,32,128]{3,2,1,0:T(8,128)S(1)} %get-tuple-element.11.refs_2_), custom_call_target="tpu_custom_call" | custom-call | tf_op jit(solution)/shard_map/pallas_call | solution.py:652
